TPU v7x, 512 devices: a whole 4x8x8 slice. The times are simulated.
512 devices in a mesh: row: 8 (over y), col: 16 (over z, core), own: 4 (over x).
Axes of the slice: x: 4, y: 8, z: 8, core: 2. Of those that a mesh axis runs over, the one named last changes fastest.
Arguments:
- viscosity: float32 [8192, 2048], P(('row', 'own'), 'col'), may hold values from 0.5 to 8
- friction: float32 [8192, 2048], P(('row', 'own'), 'col'), may hold values from 0.3 to 6
- driving: float32 [2, 8192, 2048], P(None, ('row', 'own'), 'col'), may hold values from -32 to 32
- observed: float32 [2, 8192, 2048], P(None, ('row', 'own'), 'col'), may hold values from -6 to 6
- ice_mask: int32 [8192, 2048], P(('row', 'own'), 'col'), may hold values 0 or 1
- tile_block: int32 [64, 16], P(('row', 'own'), 'col'), may hold values from 0 to 63, as said below
- owner_list: int32 [64], replicated, may hold values from 0 to 63, each once
Outputs:
- velocity: float32 [2, 8192, 2048], P(None, ('row', 'own'), 'col')
- block_gradient: float32 [4, 16, 1024], P('own')
Inputs may be any that keep to these rules, and one draw needn't show every extreme that they name: `tile_block`: tile rows 2r and 2r+1 carry the same ids; along the tile columns they run through r*2 to r*2 + 1 in order, each id on one run of consecutive tile columns of ragged length. `owner_list`: every block appears once.
All inputs are finite; a program needn't handle non-finite values. No bound on the sum of `ice_mask` on one device may be relied on, other than what follows from the above.
Results may differ from a plain program's by a relative error of at most 0.000088.
Values sent between devices are 32-bit elements; how exact they have to be, the bound alone decides.
A program may use at most 64 MiB of HBM per device.

v0:
```python
import math

import jax
import jax.numpy as jnp
from jax import lax
from jax.sharding import PartitionSpec as P

TILE = 128
MODES = 32


damping = 0.5


def from_behind(x, axis, by):
    size = lax.axis_size(axis)
    pairs = [(i, i + by) for i in range(size) if 0 <= i + by < size]
    return lax.ppermute(x, axis, pairs)


def padded_2(cells, sides, width):
    for axis, dim in sides:
        count = lax.axis_size(axis)
        ends = count - 1
        head = lax.slice_in_dim(cells, 0, width, axis=dim)
        tail = lax.slice_in_dim(cells, cells.shape[dim] - width, cells.shape[dim], axis=dim)
        cells = jnp.concatenate(
            [
                lax.ppermute(tail, axis, [(i, (i + 1) % count) for i in range(ends)]),
                cells,
                lax.ppermute(head, axis, [((i + 1) % count, i) for i in range(ends)]),
            ],
            axis=dim,
        )
    return cells


def along_x(field):
    return 0.5 * (field[1:, :-1] - field[:-1, :-1] + (field[1:, 1:] - field[:-1, 1:]))


def along_y(field):
    return 0.5 * (field[:-1, 1:] - field[:-1, :-1] + (field[1:, 1:] - field[1:, :-1]))


def back_x(corner):
    return 0.5 * (corner[:-1, :-1] + corner[:-1, 1:] - (corner[1:, :-1] + corner[1:, 1:]))


def back_y(corner):
    return 0.5 * (corner[:-1, :-1] + corner[1:, :-1] - (corner[:-1, 1:] + corner[1:, 1:]))


def apply_operator(state, viscous, friction_in):
    first_x = along_x(state[0])
    first_y = along_y(state[0])
    second_x = along_x(state[1])
    second_y = along_y(state[1])
    corner_visc = viscous[:-1, :-1]
    normal_one = corner_visc * (4.0 * first_x + 2.0 * second_y)
    shear = corner_visc * (first_y + second_x)
    normal_two = corner_visc * (4.0 * second_y + 2.0 * first_x)
    inner = state[:, 1:-1, 1:-1]
    out_first = back_x(normal_one) + back_y(shear) + friction_in * inner[0]
    out_second = back_y(normal_two) + back_x(shear) + friction_in * inner[1]
    return jnp.stack([out_first, out_second])


def diagonal_of(viscous, friction_in):
    corner = viscous[:-1, :-1]
    return (
        1.25 * (corner[:-1, :-1] + corner[:-1, 1:] + corner[1:, :-1] + corner[1:, 1:]) + friction_in
    )


def relax(state, viscous, friction_in, target, safe_diag, keep):
    inner = state[:, 1:-1, 1:-1]
    image = apply_operator(state, viscous, friction_in)
    return jnp.where(keep, inner + damping * (target - image) / safe_diag, 0.0)


def cosine_basis():
    places = jnp.arange(TILE, dtype=jnp.float32) + 0.5
    orders = jnp.arange(MODES, dtype=jnp.float32)
    return jnp.cos(math.pi * places[:, None] * orders[None, :] / TILE)


def local(viscosity, friction, driving, observed, ice_mask, tile_block, owner_list):
    keep = ice_mask > 0
    above = from_behind(viscosity[-1:, :], ("row", "own"), 1)
    extended = jnp.concatenate([above, viscosity], axis=0)
    before = from_behind(extended[:, -1:], "col", 1)
    extended = jnp.concatenate([before, extended], axis=1)
    visc_pad = jnp.pad(extended, ((0, 1), (0, 1)))
    safe_diag = jnp.where(keep, diagonal_of(visc_pad, friction), 1.0)

    def sweep_once(current, target):
        padded = padded_2(current, ((("row", "own"), 1), ("col", 2)), 1)
        return relax(padded, visc_pad, friction, target, safe_diag, keep)

    state = jnp.where(keep, driving / safe_diag, 0.0)
    for sweep_index in range(3):
        state = sweep_once(state, driving)
    misfit = jnp.where(keep, state - observed, 0.0)
    adjoint = jnp.where(keep, misfit / safe_diag, 0.0)
    for sweep_index in range(3):
        adjoint = sweep_once(adjoint, misfit)
    density = -friction * (adjoint[0] * state[0] + adjoint[1] * state[1])
    tile_cols = density.shape[1] // TILE
    tiles = density.reshape(density.shape[0] // TILE, TILE, tile_cols, TILE)
    basis = cosine_basis()
    projected = (
        jnp.einsum("ip,aicj,jq->acpq", basis, tiles, basis, precision=lax.Precision.HIGHEST) / TILE
    )
    flat = projected.reshape(-1, MODES * MODES)
    groups = owner_list.shape[0] // lax.axis_size(("row", "own"))
    local_ids = tile_block.reshape(-1) - lax.axis_index(("row", "own")) * groups
    one_hot = (local_ids[:, None] == jnp.arange(groups, dtype=jnp.int32)[None, :]).astype(
        jnp.float32
    )
    partial_value = jnp.dot(one_hot.T, flat, precision=lax.Precision.HIGHEST)
    owner_rows = owner_list.reshape(lax.axis_size("own"), -1)
    mine = lax.dynamic_index_in_dim(owner_rows, lax.axis_index("own"), 0, keepdims=False)
    summed = lax.psum(partial_value, "col")
    every = lax.all_gather(summed, ("row", "own"), axis=0, tiled=True)
    picked = jnp.take(every, mine, axis=0)
    return (state, picked[None])


def solution(mesh):
    return jax.shard_map(
        local,
        mesh=mesh,
        in_specs=(
            P(("row", "own"), "col"),
            P(("row", "own"), "col"),
            P(None, ("row", "own"), "col"),
            P(None, ("row", "own"), "col"),
            P(("row", "own"), "col"),
            P(("row", "own"), "col"),
            P(),
        ),
        out_specs=(P(None, ("row", "own"), "col"), P("own", None, None)),
        check_vma=False,
    )
```

profile of v0, /device:TPU:264, one launch (start us, length us, event | category | flops | bytes accessed | tf_op | source)
XLA Modules:
  0.0 236.5 jit_solution(6332150710618057982)
XLA Ops:
  0.6 0.7 slice.625
  1.3 3.5 %collective-permute-start = (f32[1,128]{1,0:T(1,128)S(1)}, f32[1,128]{1,0:T(1,128)S(1)}, u32[]{:S(2)}, u32[]{:S(2)}) collective-permute-start(f32[1,128]{1,0:T(1,128)S(1)} %slice.625), channel_id=1, source_target_pairs={{0,1},{1,2},{2,3},{3,64},{64,65},{65,66},{66,67},{67,128},{128,129... | collective-permute-start | bytes 1544 | tf_op jit(solution)/shard_map/ppermute | solution.py:18
  4.9 4.1 %collective-permute-done = f32[1,128]{1,0:T(1,128)S(1)} collective-permute-done((f32[1,128]{1,0:T(1,128)S(1)}, f32[1,128]{1,0:T(1,128)S(1)}, u32[]{:S(2)}, u32[]{:S(2)}) %collective-permute-start) | collective-permute-done | bytes 544 | tf_op jit(solution)/shard_map/ppermute | solution.py:18
  9.0 1.0 slice_maximum_fusion
  10.0 2.1 collective-permute-start.1
  12.1 5.6 %collective-permute-done.1 = f32[257,1]{1,0:T(8,128)S(1)} collective-permute-done((f32[257,1]{1,0:T(8,128)S(1)}, f32[257,1]{1,0:T(8,128)S(1)}, u32[]{:S(2)}, u32[]{:S(2)}) %collective-permute-start.1) | collective-permute-done | bytes 1060 | tf_op jit(solution)/shard_map/ppermute | solution.py:18
  17.9 0.9 copy-done.2
  18.9 2.4 %collective-permute-start.3 = (f32[2,1,128]{2,1,0:T(1,128)S(1)}, f32[2,1,128]{2,1,0:T(1,128)S(1)}, u32[]{:S(2)}, u32[]{:S(2)}) collective-permute-start(f32[2,1,128]{2,1,0:T(1,128)S(1)} %get-tuple-element.84), channel_id=1, source_target_pairs={{1,0},{2,1},{3,2},{64,3},{65,64},{66,65},{67,66},{128,67},{129,128... | collective-permute-start | bytes 3080 | tf_op jit(solution)/shard_map/ppermute | solution.py:31
  21.3 3.4 %collective-permute-start.2 = (f32[2,1,128]{2,1,0:T(1,128)S(1)}, f32[2,1,128]{2,1,0:T(1,128)S(1)}, u32[]{:S(2)}, u32[]{:S(2)}) collective-permute-start(f32[2,1,128]{2,1,0:T(1,128)S(1)} %get-tuple-element.83), channel_id=1, source_target_pairs={{0,1},{1,2},{2,3},{3,64},{64,65},{65,66},{66,67},{67,128},{128,129... | collective-permute-start | bytes 3080 | tf_op jit(solution)/shard_map/ppermute | solution.py:29
  24.7 4.2 %collective-permute-done.2 = f32[2,1,128]{2,1,0:T(1,128)S(1)} collective-permute-done((f32[2,1,128]{2,1,0:T(1,128)S(1)}, f32[2,1,128]{2,1,0:T(1,128)S(1)}, u32[]{:S(2)}, u32[]{:S(2)}) %collective-permute-start.2) | collective-permute-done | bytes 1056 | tf_op jit(solution)/shard_map/ppermute | solution.py:29
  29.1 1.9 collective-permute-start.5
  31.0 2.4 %collective-permute-start.4 = (f32[2,258,1]{2,1,0:T(8,128)S(1)}, f32[2,258,1]{2,1,0:T(8,128)S(1)}, u32[]{:S(2)}, u32[]{:S(2)}) collective-permute-start(f32[2,258,1]{2,1,0:T(8,128)S(1)} %get-tuple-element.59), channel_id=1, source_target_pairs={{0,4},{4,8},{8,12},{12,16},{16,20},{20,24},{24,28},{28,32},{32,36}... | collective-permute-start | bytes 6200 | tf_op jit(solution)/shard_map/ppermute | solution.py:29
  33.4 1.5 collective-permute-done.5
  34.9 5.0 %collective-permute-done.4 = f32[2,258,1]{2,1,0:T(8,128)S(1)} collective-permute-done((f32[2,258,1]{2,1,0:T(8,128)S(1)}, f32[2,258,1]{2,1,0:T(8,128)S(1)}, u32[]{:S(2)}, u32[]{:S(2)}) %collective-permute-start.4) | collective-permute-done | bytes 2096 | tf_op jit(solution)/shard_map/ppermute | solution.py:29
  40.3 0.4 add_multiply_fusion.11
  40.7 0.4 multiply_multiply_fusion.5
  41.6 1.9 collective-permute-start.7
  43.5 3.9 %collective-permute-start.6 = (f32[2,1,128]{2,1,0:T(1,128)S(1)}, f32[2,1,128]{2,1,0:T(1,128)S(1)}, u32[]{:S(2)}, u32[]{:S(2)}) collective-permute-start(f32[2,1,128]{2,1,0:T(1,128)S(1)} %get-tuple-element.81), channel_id=1, source_target_pairs={{0,1},{1,2},{2,3},{3,64},{64,65},{65,66},{66,67},{67,128},{128,129... | collective-permute-start | bytes 3080 | tf_op jit(solution)/shard_map/ppermute | solution.py:29
  47.4 3.6 %collective-permute-done.6 = f32[2,1,128]{2,1,0:T(1,128)S(1)} collective-permute-done((f32[2,1,128]{2,1,0:T(1,128)S(1)}, f32[2,1,128]{2,1,0:T(1,128)S(1)}, u32[]{:S(2)}, u32[]{:S(2)}) %collective-permute-start.6) | collective-permute-done | bytes 1056 | tf_op jit(solution)/shard_map/ppermute | solution.py:29
  51.2 1.9 collective-permute-start.9
  53.2 2.4 %collective-permute-start.8 = (f32[2,258,1]{2,1,0:T(8,128)S(1)}, f32[2,258,1]{2,1,0:T(8,128)S(1)}, u32[]{:S(2)}, u32[]{:S(2)}) collective-permute-start(f32[2,258,1]{2,1,0:T(8,128)S(1)} %get-tuple-element.57), channel_id=1, source_target_pairs={{0,4},{4,8},{8,12},{12,16},{16,20},{20,24},{24,28},{28,32},{32,36}... | collective-permute-start | bytes 6200 | tf_op jit(solution)/shard_map/ppermute | solution.py:29
  55.6 1.5 collective-permute-done.9
  57.1 5.0 %collective-permute-done.8 = f32[2,258,1]{2,1,0:T(8,128)S(1)} collective-permute-done((f32[2,258,1]{2,1,0:T(8,128)S(1)}, f32[2,258,1]{2,1,0:T(8,128)S(1)}, u32[]{:S(2)}, u32[]{:S(2)}) %collective-permute-start.8) | collective-permute-done | bytes 2096 | tf_op jit(solution)/shard_map/ppermute | solution.py:29
  62.5 0.4 add_multiply_fusion.9
  62.9 0.4 multiply_multiply_fusion.4
  63.8 1.9 collective-permute-start.11
  65.7 3.9 %collective-permute-start.10 = (f32[2,1,128]{2,1,0:T(1,128)S(1)}, f32[2,1,128]{2,1,0:T(1,128)S(1)}, u32[]{:S(2)}, u32[]{:S(2)}) collective-permute-start(f32[2,1,128]{2,1,0:T(1,128)S(1)} %get-tuple-element.79), channel_id=1, source_target_pairs={{0,1},{1,2},{2,3},{3,64},{64,65},{65,66},{66,67},{67,128},{128,129... | collective-permute-start | bytes 3080 | tf_op jit(solution)/shard_map/ppermute | solution.py:29
  69.7 3.6 %collective-permute-done.10 = f32[2,1,128]{2,1,0:T(1,128)S(1)} collective-permute-done((f32[2,1,128]{2,1,0:T(1,128)S(1)}, f32[2,1,128]{2,1,0:T(1,128)S(1)}, u32[]{:S(2)}, u32[]{:S(2)}) %collective-permute-start.10) | collective-permute-done | bytes 1056 | tf_op jit(solution)/shard_map/ppermute | solution.py:29
  73.5 1.9 collective-permute-start.13
  75.4 2.4 %collective-permute-start.12 = (f32[2,258,1]{2,1,0:T(8,128)S(1)}, f32[2,258,1]{2,1,0:T(8,128)S(1)}, u32[]{:S(2)}, u32[]{:S(2)}) collective-permute-start(f32[2,258,1]{2,1,0:T(8,128)S(1)} %get-tuple-element.55), channel_id=1, source_target_pairs={{0,4},{4,8},{8,12},{12,16},{16,20},{20,24},{24,28},{28,32},{32,36}... | collective-permute-start | bytes 6200 | tf_op jit(solution)/shard_map/ppermute | solution.py:29
  77.8 1.5 collective-permute-done.13
  79.4 5.0 %collective-permute-done.12 = f32[2,258,1]{2,1,0:T(8,128)S(1)} collective-permute-done((f32[2,258,1]{2,1,0:T(8,128)S(1)}, f32[2,258,1]{2,1,0:T(8,128)S(1)}, u32[]{:S(2)}, u32[]{:S(2)}) %collective-permute-start.12) | collective-permute-done | bytes 2096 | tf_op jit(solution)/shard_map/ppermute | solution.py:29
  84.7 0.4 add_multiply_fusion.7
  85.2 0.4 multiply_multiply_fusion.3
  85.9 0.7 copy-done.4
  86.8 1.9 collective-permute-start.15
  88.7 3.9 %collective-permute-start.14 = (f32[2,1,128]{2,1,0:T(1,128)S(1)}, f32[2,1,128]{2,1,0:T(1,128)S(1)}, u32[]{:S(2)}, u32[]{:S(2)}) collective-permute-start(f32[2,1,128]{2,1,0:T(1,128)S(1)} %get-tuple-element.77), channel_id=1, source_target_pairs={{0,1},{1,2},{2,3},{3,64},{64,65},{65,66},{66,67},{67,128},{128,129... | collective-permute-start | bytes 3080 | tf_op jit(solution)/shard_map/ppermute | solution.py:29
  92.7 3.6 %collective-permute-done.14 = f32[2,1,128]{2,1,0:T(1,128)S(1)} collective-permute-done((f32[2,1,128]{2,1,0:T(1,128)S(1)}, f32[2,1,128]{2,1,0:T(1,128)S(1)}, u32[]{:S(2)}, u32[]{:S(2)}) %collective-permute-start.14) | collective-permute-done | bytes 1056 | tf_op jit(solution)/shard_map/ppermute | solution.py:29
  96.5 1.9 collective-permute-start.17
  98.4 2.4 %collective-permute-start.16 = (f32[2,258,1]{2,1,0:T(8,128)S(1)}, f32[2,258,1]{2,1,0:T(8,128)S(1)}, u32[]{:S(2)}, u32[]{:S(2)}) collective-permute-start(f32[2,258,1]{2,1,0:T(8,128)S(1)} %get-tuple-element.53), channel_id=1, source_target_pairs={{0,4},{4,8},{8,12},{12,16},{16,20},{20,24},{24,28},{28,32},{32,36}... | collective-permute-start | bytes 6200 | tf_op jit(solution)/shard_map/ppermute | solution.py:29
  100.9 0.6 copy-done.6
  101.6 0.8 collective-permute-done.17
  102.4 5.0 %collective-permute-done.16 = f32[2,258,1]{2,1,0:T(8,128)S(1)} collective-permute-done((f32[2,258,1]{2,1,0:T(8,128)S(1)}, f32[2,258,1]{2,1,0:T(8,128)S(1)}, u32[]{:S(2)}, u32[]{:S(2)}) %collective-permute-start.16) | collective-permute-done | bytes 2096 | tf_op jit(solution)/shard_map/ppermute | solution.py:29
  108.2 0.4 multiply_multiply_fusion.2
  109.0 1.9 collective-permute-start.19
  110.9 3.9 %collective-permute-start.18 = (f32[2,1,128]{2,1,0:T(1,128)S(1)}, f32[2,1,128]{2,1,0:T(1,128)S(1)}, u32[]{:S(2)}, u32[]{:S(2)}) collective-permute-start(f32[2,1,128]{2,1,0:T(1,128)S(1)} %get-tuple-element.75), channel_id=1, source_target_pairs={{0,1},{1,2},{2,3},{3,64},{64,65},{65,66},{66,67},{67,128},{128,129... | collective-permute-start | bytes 3080 | tf_op jit(solution)/shard_map/ppermute | solution.py:29
  114.9 3.6 %collective-permute-done.18 = f32[2,1,128]{2,1,0:T(1,128)S(1)} collective-permute-done((f32[2,1,128]{2,1,0:T(1,128)S(1)}, f32[2,1,128]{2,1,0:T(1,128)S(1)}, u32[]{:S(2)}, u32[]{:S(2)}) %collective-permute-start.18) | collective-permute-done | bytes 1056 | tf_op jit(solution)/shard_map/ppermute | solution.py:29
  118.7 1.9 collective-permute-start.21
  120.6 2.4 %collective-permute-start.20 = (f32[2,258,1]{2,1,0:T(8,128)S(1)}, f32[2,258,1]{2,1,0:T(8,128)S(1)}, u32[]{:S(2)}, u32[]{:S(2)}) collective-permute-start(f32[2,258,1]{2,1,0:T(8,128)S(1)} %get-tuple-element.51), channel_id=1, source_target_pairs={{0,4},{4,8},{8,12},{12,16},{16,20},{20,24},{24,28},{28,32},{32,36}... | collective-permute-start | bytes 6200 | tf_op jit(solution)/shard_map/ppermute | solution.py:29
  123.0 1.5 collective-permute-done.21
  124.6 5.0 %collective-permute-done.20 = f32[2,258,1]{2,1,0:T(8,128)S(1)} collective-permute-done((f32[2,258,1]{2,1,0:T(8,128)S(1)}, f32[2,258,1]{2,1,0:T(8,128)S(1)}, u32[]{:S(2)}, u32[]{:S(2)}) %collective-permute-start.20) | collective-permute-done | bytes 2096 | tf_op jit(solution)/shard_map/ppermute | solution.py:29
  130.4 0.4 multiply_multiply_fusion.1
  131.2 1.9 collective-permute-start.23
  133.2 3.9 %collective-permute-start.22 = (f32[2,1,128]{2,1,0:T(1,128)S(1)}, f32[2,1,128]{2,1,0:T(1,128)S(1)}, u32[]{:S(2)}, u32[]{:S(2)}) collective-permute-start(f32[2,1,128]{2,1,0:T(1,128)S(1)} %get-tuple-element.73), channel_id=1, source_target_pairs={{0,1},{1,2},{2,3},{3,64},{64,65},{65,66},{66,67},{67,128},{128,129... | collective-permute-start | bytes 3080 | tf_op jit(solution)/shard_map/ppermute | solution.py:29
  137.1 3.6 %collective-permute-done.22 = f32[2,1,128]{2,1,0:T(1,128)S(1)} collective-permute-done((f32[2,1,128]{2,1,0:T(1,128)S(1)}, f32[2,1,128]{2,1,0:T(1,128)S(1)}, u32[]{:S(2)}, u32[]{:S(2)}) %collective-permute-start.22) | collective-permute-done | bytes 1056 | tf_op jit(solution)/shard_map/ppermute | solution.py:29
  140.9 1.9 collective-permute-start.25
  142.8 2.6 %collective-permute-start.24 = (f32[2,258,1]{2,1,0:T(8,128)S(1)}, f32[2,258,1]{2,1,0:T(8,128)S(1)}, u32[]{:S(2)}, u32[]{:S(2)}) collective-permute-start(f32[2,258,1]{2,1,0:T(8,128)S(1)} %get-tuple-element.49), channel_id=1, source_target_pairs={{0,4},{4,8},{8,12},{12,16},{16,20},{20,24},{24,28},{28,32},{32,36}... | collective-permute-start | bytes 6200 | tf_op jit(solution)/shard_map/ppermute | solution.py:29
  145.5 1.3 collective-permute-done.25
  146.8 5.0 %collective-permute-done.24 = f32[2,258,1]{2,1,0:T(8,128)S(1)} collective-permute-done((f32[2,258,1]{2,1,0:T(8,128)S(1)}, f32[2,258,1]{2,1,0:T(8,128)S(1)}, u32[]{:S(2)}, u32[]{:S(2)}) %collective-permute-start.24) | collective-permute-done | bytes 2096 | tf_op jit(solution)/shard_map/ppermute | solution.py:29
  152.6 0.4 multiply_multiply_fusion
  154.4 24.1 %psum.7 = f32[2,1024]{1,0:T(2,128)S(1)} all-reduce(f32[2,1024]{1,0:T(2,128)S(1)} %fusion.111), channel_id=1, replica_groups=mesh['row'=8,'col'=16,'own'=4] {'col'}, use_global_device_ids=true, to_apply=%region_0.1 | all-reduce | flops 2048 | bytes 16384 | tf_op jit(solution)/shard_map/psum | solution.py:124
  178.5 56.5 %all-gather = f32[32,2,1024]{2,1,0:T(2,128)S(1)} all-gather(f32[1,2,1024]{2,1,0:T(2,128)S(1)} %bitcast.169), channel_id=1, replica_groups=mesh['row'=8,'col'=16,'own'=4] {'row','own'}, dimensions={0}, use_global_device_ids=true | all-gather | bytes 270336 | tf_op jit(solution)/shard_map/all_gather | solution.py:125
  235.2 0.6 gather_fusion
  235.8 0.7 bitcast_select_fusion
  (79 shorter events, 8.2 us)
Async XLA Ops:
  1.3 16.4 %copy-start = (f32[256,128]{1,0:T(8,128)S(1)}, f32[256,128]{1,0:T(8,128)}, u32[]{:S(2)}) copy-start(f32[256,128]{1,0:T(8,128)} %param.7) | copy-start | bytes 393220
  1.3 7.7 %collective-permute-start = (f32[1,128]{1,0:T(1,128)S(1)}, f32[1,128]{1,0:T(1,128)S(1)}, u32[]{:S(2)}, u32[]{:S(2)}) collective-permute-start(f32[1,128]{1,0:T(1,128)S(1)} %slice.625), channel_id=1, source_target_pairs={{0,1},{1,2},{2,3},{3,64},{64,65},{65,66},{66,67},{67,128},{128,129... | collective-permute-start | bytes 1544 | tf_op jit(solution)/shard_map/ppermute | solution.py:18
  10.0 7.8 %copy-start.1 = (f32[256,128]{1,0:T(8,128)S(1)}, f32[256,128]{1,0:T(8,128)}, u32[]{:S(2)}) copy-start(f32[256,128]{1,0:T(8,128)} %param.8) | copy-start | bytes 393220
  10.0 7.8 %copy-start.5 = (s32[256,128]{1,0:T(8,128)S(1)}, s32[256,128]{1,0:T(8,128)}, u32[]{:S(2)}) copy-start(s32[256,128]{1,0:T(8,128)} %param.11) | copy-start | bytes 393220
  10.0 7.7 %collective-permute-start.1 = (f32[257,1]{1,0:T(8,128)S(1)}, f32[257,1]{1,0:T(8,128)S(1)}, u32[]{:S(2)}, u32[]{:S(2)}) collective-permute-start(f32[257,1]{1,0:T(8,128)S(1)} %slice_maximum_fusion), channel_id=1, source_target_pairs={{0,4},{4,8},{8,12},{12,16},{16,20},{20,24},{24,28},{28,32},{32,36}... | collective-permute-start | bytes 3092 | tf_op jit(solution)/shard_map/ppermute | solution.py:18
  17.9 1.0 copy-start.2
  18.9 5.9 %collective-permute-start.3 = (f32[2,1,128]{2,1,0:T(1,128)S(1)}, f32[2,1,128]{2,1,0:T(1,128)S(1)}, u32[]{:S(2)}, u32[]{:S(2)}) collective-permute-start(f32[2,1,128]{2,1,0:T(1,128)S(1)} %get-tuple-element.84), channel_id=1, source_target_pairs={{1,0},{2,1},{3,2},{64,3},{65,64},{66,65},{67,66},{128,67},{129,128... | collective-permute-start | bytes 3080 | tf_op jit(solution)/shard_map/ppermute | solution.py:31
  21.3 7.6 %collective-permute-start.2 = (f32[2,1,128]{2,1,0:T(1,128)S(1)}, f32[2,1,128]{2,1,0:T(1,128)S(1)}, u32[]{:S(2)}, u32[]{:S(2)}) collective-permute-start(f32[2,1,128]{2,1,0:T(1,128)S(1)} %get-tuple-element.83), channel_id=1, source_target_pairs={{0,1},{1,2},{2,3},{3,64},{64,65},{65,66},{66,67},{67,128},{128,129... | collective-permute-start | bytes 3080 | tf_op jit(solution)/shard_map/ppermute | solution.py:29
  29.1 5.9 %collective-permute-start.5 = (f32[2,258,1]{2,1,0:T(8,128)S(1)}, f32[2,258,1]{2,1,0:T(8,128)S(1)}, u32[]{:S(2)}, u32[]{:S(2)}) collective-permute-start(f32[2,258,1]{2,1,0:T(8,128)S(1)} %get-tuple-element.60), channel_id=1, source_target_pairs={{4,0},{8,4},{12,8},{16,12},{20,16},{24,20},{28,24},{32,28},{36,32}... | collective-permute-start | bytes 6200 | tf_op jit(solution)/shard_map/ppermute | solution.py:31
  31.0 9.0 %collective-permute-start.4 = (f32[2,258,1]{2,1,0:T(8,128)S(1)}, f32[2,258,1]{2,1,0:T(8,128)S(1)}, u32[]{:S(2)}, u32[]{:S(2)}) collective-permute-start(f32[2,258,1]{2,1,0:T(8,128)S(1)} %get-tuple-element.59), channel_id=1, source_target_pairs={{0,4},{4,8},{8,12},{12,16},{16,20},{20,24},{24,28},{28,32},{32,36}... | collective-permute-start | bytes 6200 | tf_op jit(solution)/shard_map/ppermute | solution.py:29
  41.6 5.9 %collective-permute-start.7 = (f32[2,1,128]{2,1,0:T(1,128)S(1)}, f32[2,1,128]{2,1,0:T(1,128)S(1)}, u32[]{:S(2)}, u32[]{:S(2)}) collective-permute-start(f32[2,1,128]{2,1,0:T(1,128)S(1)} %get-tuple-element.82), channel_id=1, source_target_pairs={{1,0},{2,1},{3,2},{64,3},{65,64},{66,65},{67,66},{128,67},{129,128... | collective-permute-start | bytes 3080 | tf_op jit(solution)/shard_map/ppermute | solution.py:31
  43.5 7.6 %collective-permute-start.6 = (f32[2,1,128]{2,1,0:T(1,128)S(1)}, f32[2,1,128]{2,1,0:T(1,128)S(1)}, u32[]{:S(2)}, u32[]{:S(2)}) collective-permute-start(f32[2,1,128]{2,1,0:T(1,128)S(1)} %get-tuple-element.81), channel_id=1, source_target_pairs={{0,1},{1,2},{2,3},{3,64},{64,65},{65,66},{66,67},{67,128},{128,129... | collective-permute-start | bytes 3080 | tf_op jit(solution)/shard_map/ppermute | solution.py:29
  51.2 5.9 %collective-permute-start.9 = (f32[2,258,1]{2,1,0:T(8,128)S(1)}, f32[2,258,1]{2,1,0:T(8,128)S(1)}, u32[]{:S(2)}, u32[]{:S(2)}) collective-permute-start(f32[2,258,1]{2,1,0:T(8,128)S(1)} %get-tuple-element.58), channel_id=1, source_target_pairs={{4,0},{8,4},{12,8},{16,12},{20,16},{24,20},{28,24},{32,28},{36,32}... | collective-permute-start | bytes 6200 | tf_op jit(solution)/shard_map/ppermute | solution.py:31
  53.2 9.0 %collective-permute-start.8 = (f32[2,258,1]{2,1,0:T(8,128)S(1)}, f32[2,258,1]{2,1,0:T(8,128)S(1)}, u32[]{:S(2)}, u32[]{:S(2)}) collective-permute-start(f32[2,258,1]{2,1,0:T(8,128)S(1)} %get-tuple-element.57), channel_id=1, source_target_pairs={{0,4},{4,8},{8,12},{12,16},{16,20},{20,24},{24,28},{28,32},{32,36}... | collective-permute-start | bytes 6200 | tf_op jit(solution)/shard_map/ppermute | solution.py:29
  63.8 5.9 %collective-permute-start.11 = (f32[2,1,128]{2,1,0:T(1,128)S(1)}, f32[2,1,128]{2,1,0:T(1,128)S(1)}, u32[]{:S(2)}, u32[]{:S(2)}) collective-permute-start(f32[2,1,128]{2,1,0:T(1,128)S(1)} %get-tuple-element.80), channel_id=1, source_target_pairs={{1,0},{2,1},{3,2},{64,3},{65,64},{66,65},{67,66},{128,67},{129,128... | collective-permute-start | bytes 3080 | tf_op jit(solution)/shard_map/ppermute | solution.py:31
  65.7 7.6 %collective-permute-start.10 = (f32[2,1,128]{2,1,0:T(1,128)S(1)}, f32[2,1,128]{2,1,0:T(1,128)S(1)}, u32[]{:S(2)}, u32[]{:S(2)}) collective-permute-start(f32[2,1,128]{2,1,0:T(1,128)S(1)} %get-tuple-element.79), channel_id=1, source_target_pairs={{0,1},{1,2},{2,3},{3,64},{64,65},{65,66},{66,67},{67,128},{128,129... | collective-permute-start | bytes 3080 | tf_op jit(solution)/shard_map/ppermute | solution.py:29
  73.5 5.9 %collective-permute-start.13 = (f32[2,258,1]{2,1,0:T(8,128)S(1)}, f32[2,258,1]{2,1,0:T(8,128)S(1)}, u32[]{:S(2)}, u32[]{:S(2)}) collective-permute-start(f32[2,258,1]{2,1,0:T(8,128)S(1)} %get-tuple-element.56), channel_id=1, source_target_pairs={{4,0},{8,4},{12,8},{16,12},{20,16},{24,20},{28,24},{32,28},{36,32}... | collective-permute-start | bytes 6200 | tf_op jit(solution)/shard_map/ppermute | solution.py:31
  75.4 9.0 %collective-permute-start.12 = (f32[2,258,1]{2,1,0:T(8,128)S(1)}, f32[2,258,1]{2,1,0:T(8,128)S(1)}, u32[]{:S(2)}, u32[]{:S(2)}) collective-permute-start(f32[2,258,1]{2,1,0:T(8,128)S(1)} %get-tuple-element.55), channel_id=1, source_target_pairs={{0,4},{4,8},{8,12},{12,16},{16,20},{20,24},{24,28},{28,32},{32,36}... | collective-permute-start | bytes 6200 | tf_op jit(solution)/shard_map/ppermute | solution.py:29
  85.6 1.0 copy-start.4
  86.8 66.7 %copy-start.3 = (f32[2,256,128]{2,1,0:T(8,128)}, f32[2,256,128]{2,1,0:T(8,128)S(1)}, u32[]{:S(2)}) copy-start(f32[2,256,128]{2,1,0:T(8,128)S(1)} %get-tuple-element.13) | copy-start | bytes 786436
  86.8 5.9 %collective-permute-start.15 = (f32[2,1,128]{2,1,0:T(1,128)S(1)}, f32[2,1,128]{2,1,0:T(1,128)S(1)}, u32[]{:S(2)}, u32[]{:S(2)}) collective-permute-start(f32[2,1,128]{2,1,0:T(1,128)S(1)} %get-tuple-element.78), channel_id=1, source_target_pairs={{1,0},{2,1},{3,2},{64,3},{65,64},{66,65},{67,66},{128,67},{129,128... | collective-permute-start | bytes 3080 | tf_op jit(solution)/shard_map/ppermute | solution.py:31
  88.7 7.6 %collective-permute-start.14 = (f32[2,1,128]{2,1,0:T(1,128)S(1)}, f32[2,1,128]{2,1,0:T(1,128)S(1)}, u32[]{:S(2)}, u32[]{:S(2)}) collective-permute-start(f32[2,1,128]{2,1,0:T(1,128)S(1)} %get-tuple-element.77), channel_id=1, source_target_pairs={{0,1},{1,2},{2,3},{3,64},{64,65},{65,66},{66,67},{67,128},{128,129... | collective-permute-start | bytes 3080 | tf_op jit(solution)/shard_map/ppermute | solution.py:29
  96.5 4.4 %copy-start.7 = (s32[2,1]{0,1:T(1,128)S(1)}, s32[2,1]{0,1:T(1,128)}, u32[]{:S(2)}) copy-start(s32[2,1]{0,1:T(1,128)} %param.12) | copy-start | bytes 28
  96.5 5.9 %collective-permute-start.17 = (f32[2,258,1]{2,1,0:T(8,128)S(1)}, f32[2,258,1]{2,1,0:T(8,128)S(1)}, u32[]{:S(2)}, u32[]{:S(2)}) collective-permute-start(f32[2,258,1]{2,1,0:T(8,128)S(1)} %get-tuple-element.54), channel_id=1, source_target_pairs={{4,0},{8,4},{12,8},{16,12},{20,16},{24,20},{28,24},{32,28},{36,32}... | collective-permute-start | bytes 6200 | tf_op jit(solution)/shard_map/ppermute | solution.py:31
  98.4 9.0 %collective-permute-start.16 = (f32[2,258,1]{2,1,0:T(8,128)S(1)}, f32[2,258,1]{2,1,0:T(8,128)S(1)}, u32[]{:S(2)}, u32[]{:S(2)}) collective-permute-start(f32[2,258,1]{2,1,0:T(8,128)S(1)} %get-tuple-element.53), channel_id=1, source_target_pairs={{0,4},{4,8},{8,12},{12,16},{16,20},{20,24},{24,28},{28,32},{32,36}... | collective-permute-start | bytes 6200 | tf_op jit(solution)/shard_map/ppermute | solution.py:29
  100.8 0.7 copy-start.6
  109.0 5.9 %collective-permute-start.19 = (f32[2,1,128]{2,1,0:T(1,128)S(1)}, f32[2,1,128]{2,1,0:T(1,128)S(1)}, u32[]{:S(2)}, u32[]{:S(2)}) collective-permute-start(f32[2,1,128]{2,1,0:T(1,128)S(1)} %get-tuple-element.76), channel_id=1, source_target_pairs={{1,0},{2,1},{3,2},{64,3},{65,64},{66,65},{67,66},{128,67},{129,128... | collective-permute-start | bytes 3080 | tf_op jit(solution)/shard_map/ppermute | solution.py:31
  110.9 7.6 %collective-permute-start.18 = (f32[2,1,128]{2,1,0:T(1,128)S(1)}, f32[2,1,128]{2,1,0:T(1,128)S(1)}, u32[]{:S(2)}, u32[]{:S(2)}) collective-permute-start(f32[2,1,128]{2,1,0:T(1,128)S(1)} %get-tuple-element.75), channel_id=1, source_target_pairs={{0,1},{1,2},{2,3},{3,64},{64,65},{65,66},{66,67},{67,128},{128,129... | collective-permute-start | bytes 3080 | tf_op jit(solution)/shard_map/ppermute | solution.py:29
  118.7 5.9 %collective-permute-start.21 = (f32[2,258,1]{2,1,0:T(8,128)S(1)}, f32[2,258,1]{2,1,0:T(8,128)S(1)}, u32[]{:S(2)}, u32[]{:S(2)}) collective-permute-start(f32[2,258,1]{2,1,0:T(8,128)S(1)} %get-tuple-element.52), channel_id=1, source_target_pairs={{4,0},{8,4},{12,8},{16,12},{20,16},{24,20},{28,24},{32,28},{36,32}... | collective-permute-start | bytes 6200 | tf_op jit(solution)/shard_map/ppermute | solution.py:31
  120.6 9.0 %collective-permute-start.20 = (f32[2,258,1]{2,1,0:T(8,128)S(1)}, f32[2,258,1]{2,1,0:T(8,128)S(1)}, u32[]{:S(2)}, u32[]{:S(2)}) collective-permute-start(f32[2,258,1]{2,1,0:T(8,128)S(1)} %get-tuple-element.51), channel_id=1, source_target_pairs={{0,4},{4,8},{8,12},{12,16},{16,20},{20,24},{24,28},{28,32},{32,36}... | collective-permute-start | bytes 6200 | tf_op jit(solution)/shard_map/ppermute | solution.py:29
  131.2 5.9 %collective-permute-start.23 = (f32[2,1,128]{2,1,0:T(1,128)S(1)}, f32[2,1,128]{2,1,0:T(1,128)S(1)}, u32[]{:S(2)}, u32[]{:S(2)}) collective-permute-start(f32[2,1,128]{2,1,0:T(1,128)S(1)} %get-tuple-element.74), channel_id=1, source_target_pairs={{1,0},{2,1},{3,2},{64,3},{65,64},{66,65},{67,66},{128,67},{129,128... | collective-permute-start | bytes 3080 | tf_op jit(solution)/shard_map/ppermute | solution.py:31
  133.2 7.6 %collective-permute-start.22 = (f32[2,1,128]{2,1,0:T(1,128)S(1)}, f32[2,1,128]{2,1,0:T(1,128)S(1)}, u32[]{:S(2)}, u32[]{:S(2)}) collective-permute-start(f32[2,1,128]{2,1,0:T(1,128)S(1)} %get-tuple-element.73), channel_id=1, source_target_pairs={{0,1},{1,2},{2,3},{3,64},{64,65},{65,66},{66,67},{67,128},{128,129... | collective-permute-start | bytes 3080 | tf_op jit(solution)/shard_map/ppermute | solution.py:29
  140.9 5.9 %collective-permute-start.25 = (f32[2,258,1]{2,1,0:T(8,128)S(1)}, f32[2,258,1]{2,1,0:T(8,128)S(1)}, u32[]{:S(2)}, u32[]{:S(2)}) collective-permute-start(f32[2,258,1]{2,1,0:T(8,128)S(1)} %get-tuple-element.50), channel_id=1, source_target_pairs={{4,0},{8,4},{12,8},{16,12},{20,16},{24,20},{28,24},{32,28},{36,32}... | collective-permute-start | bytes 6200 | tf_op jit(solution)/shard_map/ppermute | solution.py:31
  142.8 9.0 %collective-permute-start.24 = (f32[2,258,1]{2,1,0:T(8,128)S(1)}, f32[2,258,1]{2,1,0:T(8,128)S(1)}, u32[]{:S(2)}, u32[]{:S(2)}) collective-permute-start(f32[2,258,1]{2,1,0:T(8,128)S(1)} %get-tuple-element.49), channel_id=1, source_target_pairs={{0,4},{4,8},{8,12},{12,16},{16,20},{20,24},{24,28},{28,32},{32,36}... | collective-permute-start | bytes 6200 | tf_op jit(solution)/shard_map/ppermute | solution.py:29
where the time goes:
time: 238 us; the launch traced here: 236 us
  blocking collectives  80.5 us (34%)
  waiting for transfers between devices  70.5 us (30%)
  starting transfers between devices  66.8 us (28%)
  other arithmetic  11.6 us (5%)
  local copies, waits for them, and re-layouts  4.87 us (2%)
    all_gather x1, blocking collectives, local(): every = lax.all_gather(summed, ('row', 'own'), axis=0, tiled=True)  56.5 us
    ppermute x12, waiting for transfers between devices, padded_2(): lax.ppermute(tail, axis, [(i, (i + 1) % count) for i in range(ends)])  52.5 us
    ppermute x12, starting transfers between devices, padded_2(): lax.ppermute(tail, axis, [(i, (i + 1) % count) for i in range(ends)])  37.6 us
    psum x1, blocking collectives, local(): summed = lax.psum(partial_value, 'col')  24.1 us
    ppermute x12, starting transfers between devices, padded_2(): lax.ppermute(head, axis, [((i + 1) % count, i) for i in range(ends)])  23.6 us
    ppermute x2, waiting for transfers between devices, from_behind(): return lax.ppermute(x, axis, pairs)  9.75 us
    ppermute x12, waiting for transfers between devices, padded_2(): lax.ppermute(head, axis, [((i + 1) % count, i) for i in range(ends)])  8.29 us
    ppermute x2, starting transfers between devices, from_behind(): return lax.ppermute(x, axis, pairs)  5.57 us
  transfers between devices with their start and end apart: 26, of which 20 were waited for; matrix products, arithmetic and copies ran while one was open for 0% of the time, Pallas kernels for 0%

commit v1 on v0

v1 whole, which is shorter than its diff:
```python
import functools
import math

import jax
import jax.numpy as jnp
import numpy as np
from jax import lax
from jax.experimental import pallas as pl
from jax.experimental.pallas import tpu as pltpu
from jax.sharding import PartitionSpec as P

TILE = 128
MODES = 32
LANES = 128
HALO = 8
FIELDS = 7
SWEEPS = 3
MESH = pl.DeviceIdType.MESH
HIGHEST = lax.Precision.HIGHEST


def bases(chunks):
    per = MODES // chunks
    places = np.arange(TILE) + 0.5
    orders = np.arange(MODES)
    cosine = np.cos(math.pi * orders[:, None] * places[None, :] / TILE)
    first = np.concatenate([cosine[s::per] for s in range(per)], axis=0)
    second = np.zeros((per * TILE, LANES))
    for s in range(per):
        for group in range(2):
            at = group * per * MODES + s * MODES
            second[s * TILE : (s + 1) * TILE, at : at + MODES] = cosine.T / TILE
    return first.astype(np.float32), second.astype(np.float32)


def kernel(
    sizes,
    visc,
    fric,
    drv,
    obs,
    mask,
    tile_block,
    owner_list,
    basis_1,
    basis_2,
    vel,
    grad,
    fm,
    mk,
    fs,
    pack,
    pack_t,
    recv_t,
    diag,
    coef,
    hb,
    w,
    v,
    dens,
    b1,
    b2,
    tb,
    ol,
    send_a,
    recv_a,
    table,
    recv_c,
    out,
    load_sem,
    halo_send,
    halo_recv,
    phase_send,
    phase_recv,
    out_sem,
):
    n_row, n_own, n_col = sizes
    n_line = n_row * n_own
    rows = visc.shape[0]
    chunks = (rows + 2 * HALO) // 8
    row_at, own_at, col = (
        lax.axis_index("row"),
        lax.axis_index("own"),
        lax.axis_index("col"),
    )
    line = row_at * n_own + own_at

    def device(line_to, col_to):
        return {
            "row": lax.div(line_to, n_own),
            "own": lax.rem(line_to, n_own),
            "col": col_to,
        }

    def line_by(step):
        return lax.rem(line + (step + n_line), n_line)

    def col_by(step):
        return lax.rem(col + (step + n_col), n_col)

    barrier = pltpu.get_barrier_semaphore()

    def greet(line_to, col_to):
        pl.semaphore_signal(
            barrier, inc=1, device_id=device(line_to, col_to), device_id_type=MESH
        )

    for up in (-1, 1):
        for side in (-1, 1):
            greet(line_by(up), col_by(side))

    def greet_col(i, _):
        greet(line, col_by(i))
        return 0

    def greet_line(i, _):
        greet(line_by(i), col)
        return 0

    lax.fori_loop(1, n_col, greet_col, 0)
    lax.fori_loop(1, n_line, greet_line, 0)

    own_rows = pl.ds(HALO, rows)
    loads = [
        (visc, fm.at[0, own_rows, :]),
        (fric, fm.at[1, own_rows, :]),
        (drv, fm.at[2:4, own_rows, :]),
        (obs, fm.at[4:6, own_rows, :]),
        (mask, mk.at[own_rows, :]),
        (basis_1, b1),
        (basis_2, b2),
        (tile_block, tb),
        (owner_list, ol),
    ]
    loads = [
        pltpu.make_async_copy(src, dst, load_sem.at[i])
        for i, (src, dst) in enumerate(loads)
    ]
    for copy in loads:
        copy.start()

    pl.semaphore_wait(barrier, 4 + (n_col - 1) + (n_line - 1))

    lane = lax.broadcasted_iota(jnp.int32, (8, LANES), 1)
    sub = lax.broadcasted_iota(jnp.int32, (8, LANES), 0)
    last_lane, first_lane, first_sub = lane == LANES - 1, lane == 0, sub == 0

    copies = []

    def send(src, dst, line_to, col_to):
        at = len(copies)
        copy = pltpu.make_async_remote_copy(
            src_ref=src,
            dst_ref=dst,
            send_sem=halo_send.at[at],
            recv_sem=halo_recv.at[at],
            device_id=device(line_to, col_to),
            device_id_type=MESH,
        )
        copy.start()
        copies.append(copy)

    for step, source, target in (
        (-1, 0, HALO + rows),
        (1, rows - HALO, 0),
    ):
        to, take = pl.ds(target, HALO), pl.ds(source, HALO)
        send(visc.at[take, :], fm.at[0, to, :], line_by(step), col)
        send(fric.at[take, :], fm.at[1, to, :], line_by(step), col)
        send(drv.at[:, take, :], fm.at[2:4, to, :], line_by(step), col)
        send(obs.at[:, take, :], fm.at[4:6, to, :], line_by(step), col)
        send(mask.at[take, :], mk.at[to, :], line_by(step), col)

    for copy in loads[:5]:
        copy.wait()

    for t in range(rows // 8):
        at = pl.ds(HALO + 8 * t, 8)
        packed = pltpu.roll(fm[0, at, :], 8, 1)
        for f in range(1, FIELDS):
            piece = fm[f, at, :] if f < 6 else mk[at, :].astype(jnp.float32)
            packed = jnp.where(lane < 16 * f, packed, pltpu.roll(piece, 16 * f + 8, 1))
        pack[8 * t : 8 * t + 8, :] = packed

    for up, source, slot in ((-1, 0, 2), (1, rows - 8, 0)):
        for side in (-1, 1):
            send(
                pack.at[pl.ds(source, 8), :],
                diag.at[slot + (1 if side < 0 else 0)],
                line_by(up),
                col_by(side),
            )

    for part in range(rows // LANES):
        block = pack[part * LANES : (part + 1) * LANES, :]
        pack_t[:, :, part * LANES : (part + 1) * LANES] = block.T.reshape(8, 16, LANES)
    recv_t[FIELDS, :, :] = jnp.zeros((16, rows), jnp.float32)
    send(
        pack_t.at[0:FIELDS, 0:8, :],
        recv_t.at[0:FIELDS, 0:8, :],
        line,
        col_by(1),
    )
    send(
        pack_t.at[0:FIELDS, 8:16, :],
        recv_t.at[0:FIELDS, 8:16, :],
        line,
        col_by(-1),
    )

    for copy in copies:
        copy.wait_recv()

    def unpack(at, packed):
        for f in range(FIELDS):
            fs[f, at, :] = pltpu.roll(packed, LANES - (16 * f + 8), 1)

    from_left = lax.rem(lane, 16) < 8
    unpack(pl.ds(0, 8), jnp.where(from_left, diag[0], diag[1]))
    unpack(pl.ds(HALO + rows, 8), jnp.where(from_left, diag[2], diag[3]))
    for part in range(rows // LANES):
        turned = (
            recv_t[:, :, part * LANES : (part + 1) * LANES].reshape(LANES, LANES).T
        )
        for t in range(LANES // 8):
            unpack(
                pl.ds(HALO + part * LANES + 8 * t, 8), turned[8 * t : 8 * t + 8, :]
            )

    def plus(x):
        a, b = pltpu.roll(x[0], LANES - 1, 1), pltpu.roll(x[1], LANES - 1, 1)
        return jnp.where(last_lane, b, a), jnp.where(last_lane, a, b)

    def minus(x):
        a, b = pltpu.roll(x[0], 1, 1), pltpu.roll(x[1], 1, 1)
        return jnp.where(first_lane, b, a), jnp.where(first_lane, a, b)

    def both(fn, *args):
        return tuple(fn(*parts) for parts in zip(*args))

    def down(x, kept):
        turned = tuple(pltpu.roll(part, 1, 0) for part in x)
        moved = both(lambda k, r: jnp.where(first_sub, k, r), kept, turned)
        return moved, turned

    side_inside = ((lane < 64) & (col < n_col - 1)) | ((lane >= 64) & (col > 0))
    zero = jnp.zeros((8, LANES), jnp.float32)
    kept = (zero, zero)
    for t in range(chunks):
        at = pl.ds(8 * t, 8)
        n = (fm[0, at, :], fs[0, at, :])
        ice = (mk[at, :] > 0, fs[6, at, :] > 0.5)
        inside = (None, side_inside)
        if t == 0 or t == chunks - 1:
            there = line > 0 if t == 0 else line < n_line - 1
            inside = (jnp.broadcast_to(there, (8, LANES)), side_inside & there)
            n = (jnp.where(inside[0], n[0], 0.0), n[1])
            ice = (ice[0] & inside[0], ice[1])
        n = (n[0], jnp.where(inside[1], n[1], 0.0))
        ice = (ice[0], ice[1] & inside[1])
        summed = both(lambda x, y: x + y, n, minus(n))
        moved, kept = down(summed, kept)
        for i, source in ((0, fm), (1, fs)):
            f = source[1, at, :]
            half = jnp.where(
                ice[i], 0.5 / (1.25 * (summed[i] + moved[i]) + f), 0.0
            )
            coef[i, 0, at, :] = 0.5 * n[i]
            coef[i, 1, at, :] = 0.25 * n[i]
            coef[i, 2, at, :] = half
            coef[i, 3, at, :] = 1.0 - half * f
            for k in range(2):
                scaled = half * source[2 + k, at, :]
                hb[i, k, at, :] = scaled
                w[i, k, at, :] = scaled + scaled
    for i in range(2):
        for k in range(2):
            w[i, k, 8 * chunks : 8 * chunks + 8, :] = zero

    def sweep(s, _):
        @pl.when(s == SWEEPS)
        def _():
            for t in range(chunks):
                at = pl.ds(8 * t, 8)
                for i, source in ((0, fm), (1, fs)):
                    for k in range(2):
                        now = w[i, k, at, :]
                        if i == 0 and 0 < t < chunks - 1:
                            v[k, 8 * t - HALO : 8 * t - HALO + 8, :] = now
                        scaled = coef[i, 2, at, :] * (now - source[4 + k, at, :])
                        hb[i, k, at, :] = scaled
                        w[i, k, at, :] = scaled + scaled

        kept = [(zero, zero), (zero, zero)]
        for t in range(chunks):
            at, after = pl.ds(8 * t, 8), pl.ds(8 * t + 1, 8)
            now, dx, dy = [], [], []
            for k in range(2):
                here = (w[0, k, at, :], w[1, k, at, :])
                ahead = (w[0, k, after, :], w[1, k, after, :])
                e = both(lambda a, b: a - b, ahead, here)
                f = both(lambda a, b: a + b, ahead, here)
                now.append(here)
                dx.append(both(lambda a, b: a + b, e, plus(e)))
                dy.append(both(lambda a, b: a - b, plus(f), f))
            m = (coef[0, 0, at, :], coef[1, 0, at, :])
            q = (coef[0, 1, at, :], coef[1, 1, at, :])
            s_xy = both(lambda a, b: a + b, dx[0], dy[1])
            one = both(lambda a, b, c: a * (b + c), m, s_xy, dx[0])
            two = both(lambda a, b, c: a * (b + c), m, s_xy, dy[1])
            shear = both(lambda a, b, c: a * (b + c), q, dy[0], dx[1])
            one_m, two_m, shear_m = minus(one), minus(two), minus(shear)
            s_one = both(lambda a, b: a + b, one, one_m)
            d_two = both(lambda a, b: a - b, two_m, two)
            s_shear = both(lambda a, b: a + b, shear, shear_m)
            d_shear = both(lambda a, b: a - b, shear_m, shear)
            before = (
                both(lambda a, b: a + b, s_one, d_shear),
                both(lambda a, b: a + b, d_two, s_shear),
            )
            behind = (
                both(lambda a, b: a - b, d_shear, s_one),
                both(lambda a, b: a - b, d_two, s_shear),
            )
            for k in range(2):
                moved, kept[k] = down(before[k], kept[k])
                for i in range(2):
                    image = moved[i] + behind[k][i]
                    w[i, k, at, :] = (
                        coef[i, 3, at, :] * now[k][i] + hb[i, k, at, :]
                    ) - coef[i, 2, at, :] * image
        return 0

    lax.fori_loop(0, 2 * SWEEPS, sweep, 0)

    vel_copy = pltpu.make_async_copy(v, vel, out_sem.at[0])
    vel_copy.start()

    for t in range(TILE // 8):
        total = None
        for start in range(0, rows, TILE):
            at = pl.ds(start + 8 * t, 8)
            ext = pl.ds(HALO + start + 8 * t, 8)
            piece = fm[1, ext, :] * (
                w[0, 0, ext, :] * v[0, at, :] + w[0, 1, ext, :] * v[1, at, :]
            )
            total = piece if total is None else total + piece
        dens[8 * t : 8 * t + 8, :] = -total

    for copy in loads[5:]:
        copy.wait()
    per = MODES // n_col
    half_row = jnp.dot(
        b1[...], dens[...], precision=HIGHEST, preferred_element_type=jnp.float32
    )
    half_row = jnp.concatenate(
        [half_row[s * n_col : (s + 1) * n_col] for s in range(per)], axis=1
    )
    part = jnp.dot(
        half_row, b2[...], precision=HIGHEST, preferred_element_type=jnp.float32
    )
    group = tb[0, 0] - 2 * line
    wide = lax.broadcasted_iota(jnp.int32, (n_col, LANES), 1)
    part = jnp.where((wide >= 64) == (group > 0), part, 0.0)
    for i in range(n_col):
        send_a[i] = part[i : i + 1, :]

    def spread(phase, src, dst, count, to):
        def start(i, _):
            line_to, col_to, index = to(i)
            pltpu.make_async_remote_copy(
                src_ref=src(index),
                dst_ref=dst,
                send_sem=phase_send.at[phase],
                recv_sem=phase_recv.at[phase],
                device_id=device(line_to, col_to),
                device_id_type=MESH,
            ).start()
            return 0

        lax.fori_loop(1, count, start, 0)

    def arrived(phase, ref):
        pltpu.make_async_copy(ref, ref, phase_recv.at[phase]).wait()

    def departed(phase, ref):
        pltpu.make_async_copy(ref, ref, phase_send.at[phase]).wait()

    spread(
        0,
        lambda i: send_a.at[i],
        recv_a.at[col],
        n_col,
        lambda i: (line, col_by(i), col_by(i)),
    )
    recv_a[col] = send_a[col]
    arrived(0, recv_a.at[0 : n_col - 1])
    total = recv_a[0]
    for i in range(1, n_col):
        total = total + recv_a[i]

    table[line] = total
    spread(
        1,
        lambda i: table.at[line],
        table.at[line],
        n_line,
        lambda i: (line_by(i), col, i),
    )
    arrived(1, table.at[0 : n_line - 1])

    per_owner = ol.shape[0] // n_own
    left_half = lax.broadcasted_iota(jnp.int32, (1, LANES), 1) < 64
    for k in range(per_owner // 2):
        found = []
        for j in range(2):
            block = ol[own_at * per_owner + k + j * (per_owner // 2)]
            entry = table[lax.shift_right_logical(block, 1)]
            turn = lax.bitwise_and(block, 1) != j
            found.append(jnp.where(turn, pltpu.roll(entry, 64, 1), entry))
        recv_c[col, k : k + 1, :] = jnp.where(left_half, found[0], found[1])

    spread(
        2,
        lambda i: recv_c.at[col],
        recv_c.at[col],
        n_col,
        lambda i: (line, col_by(i), i),
    )
    arrived(2, recv_c.at[0 : n_col - 1])
    for z in range(n_col // 2):
        at = pl.ds(z * LANES, LANES)
        a, b = recv_c[2 * z], recv_c[2 * z + 1]
        out[0:8, at] = jnp.where(lane < 64, a, pltpu.roll(b, 64, 1))
        out[8:16, at] = jnp.where(lane < 64, pltpu.roll(a, 64, 1), b)
    grad_copy = pltpu.make_async_copy(out, grad.at[0], out_sem.at[1])
    grad_copy.start()

    for copy in copies:
        copy.wait_send()
    departed(0, recv_a.at[0 : n_col - 1])
    departed(1, table.at[0 : n_line - 1])
    departed(2, recv_c.at[0 : n_col - 1])
    vel_copy.wait()
    grad_copy.wait()


def solution(mesh):
    sizes = tuple(mesh.shape[a] for a in ("row", "own", "col"))
    n_line, n_col = sizes[0] * sizes[1], sizes[2]

    def local(viscosity, friction, driving, observed, ice_mask, tile_block, owner_list):
        rows = viscosity.shape[0]
        ext = rows + 2 * HALO
        first, second = bases(n_col)
        per_owner = owner_list.shape[0] // sizes[1]
        f32 = jnp.float32
        vmem = pltpu.VMEM
        return pl.pallas_call(
            functools.partial(kernel, sizes),
            out_shape=(
                jax.ShapeDtypeStruct((2, rows, LANES), f32),
                jax.ShapeDtypeStruct((1, per_owner, MODES * MODES), f32),
            ),
            in_specs=[pl.BlockSpec(memory_space=pltpu.HBM)] * 9,
            out_specs=[pl.BlockSpec(memory_space=pl.ANY)] * 2,
            scratch_shapes=[
                vmem((6, ext, LANES), f32),
                vmem((ext, LANES), jnp.int32),
                vmem((FIELDS, ext, LANES), f32),
                vmem((rows, LANES), f32),
                vmem((8, 16, rows), f32),
                vmem((8, 16, rows), f32),
                vmem((4, 8, LANES), f32),
                vmem((2, 4, ext, LANES), f32),
                vmem((2, 2, ext, LANES), f32),
                vmem((2, 2, ext + 8, LANES), f32),
                vmem((2, rows, LANES), f32),
                vmem((TILE, LANES), f32),
                vmem(first.shape, f32),
                vmem(second.shape, f32),
                pltpu.SMEM(tile_block.shape, jnp.int32),
                pltpu.SMEM(owner_list.shape, jnp.int32),
                vmem((n_col, 1, LANES), f32),
                vmem((n_col, 1, LANES), f32),
                vmem((n_line, 1, LANES), f32),
                vmem((n_col, 8, LANES), f32),
                vmem((per_owner, MODES * MODES), f32),
                pltpu.SemaphoreType.DMA((9,)),
                pltpu.SemaphoreType.DMA((16,)),
                pltpu.SemaphoreType.DMA((16,)),
                pltpu.SemaphoreType.DMA((3,)),
                pltpu.SemaphoreType.DMA((3,)),
                pltpu.SemaphoreType.DMA((2,)),
            ],
            compiler_params=pltpu.CompilerParams(
                collective_id=0,
                has_side_effects=True,
                vmem_limit_bytes=32 * 2**20,
            ),
        )(
            viscosity,
            friction,
            driving,
            observed,
            ice_mask,
            tile_block,
            owner_list,
            jnp.asarray(first),
            jnp.asarray(second),
        )

    return jax.shard_map(
        local,
        mesh=mesh,
        in_specs=(
            P(("row", "own"), "col"),
            P(("row", "own"), "col"),
            P(None, ("row", "own"), "col"),
            P(None, ("row", "own"), "col"),
            P(("row", "own"), "col"),
            P(("row", "own"), "col"),
            P(),
        ),
        out_specs=(P(None, ("row", "own"), "col"), P("own", None, None)),
        check_vma=False,
    )
```

time: 238 us -> 61.3 us (0.26)
  the two profiles are of different devices: /device:TPU:264 before, /device:TPU:1 now
where the time goes in v1:
time: 61.3 us; the launch traced here: 61 us
  Pallas kernels  52 us (85%)
  local copies, waits for them, and re-layouts  8.32 us (14%)
  between operations  0.65 us (1%)
    pallas_call x1, Pallas kernels, local(): pl.pallas_call(functools.partial(kernel, sizes), out_shape=(jax.ShapeDtyp...  52 us
    unnamed x19, local copies, waits for them, and re-layouts  8.32 us

profile of v1, /device:TPU:1, one launch (start us, length us, event | category | flops | bytes accessed | tf_op | source)
XLA Modules:
  0.0 61.0 jit_solution(463101642314996533)
XLA Ops:
  0.6 0.0 copy-start.7
  0.6 0.7 %copy.11.tile_block = s32[2,1]{1,0:T(2,128)S(1)} copy(s32[2,1]{0,1:T(1,128)} %param.14) | data formatting | bytes 16 | tf_op args[5]
  1.4 0.0 copy-done.7
  1.4 0.0 copy-start
  1.4 0.9 %copy-done = f32[2,256,128]{2,1,0:T(8,128)S(1)} copy-done((f32[2,256,128]{2,1,0:T(8,128)S(1)}, f32[2,256,128]{2,1,0:T(8,128)}, u32[]{:S(2)}) %copy-start) | copy-done | bytes 262168
  2.3 0.0 copy-start.1
  2.3 0.9 %copy-done.1 = f32[2,256,128]{2,1,0:T(8,128)S(1)} copy-done((f32[2,256,128]{2,1,0:T(8,128)S(1)}, f32[2,256,128]{2,1,0:T(8,128)}, u32[]{:S(2)}) %copy-start.1) | copy-done | bytes 262168
  3.3 0.0 copy-start.2
  3.3 0.9 %copy-done.2 = f32[256,128]{1,0:T(8,128)S(1)} copy-done((f32[256,128]{1,0:T(8,128)S(1)}, f32[256,128]{1,0:T(8,128)}, u32[]{:S(2)}) %copy-start.2) | copy-done | bytes 131096
  4.2 0.0 copy-start.3
  4.2 0.9 %copy-done.3 = f32[256,128]{1,0:T(8,128)S(1)} copy-done((f32[256,128]{1,0:T(8,128)S(1)}, f32[256,128]{1,0:T(8,128)}, u32[]{:S(2)}) %copy-start.3) | copy-done | bytes 131096
  5.1 0.0 copy-start.4
  5.1 0.9 %copy-done.4 = s32[256,128]{1,0:T(8,128)S(1)} copy-done((s32[256,128]{1,0:T(8,128)S(1)}, s32[256,128]{1,0:T(8,128)}, u32[]{:S(2)}) %copy-start.4) | copy-done | bytes 131096
  6.0 0.0 copy-start.5
  6.0 0.9 %copy-done.5 = f32[256,128]{1,0:T(8,128)S(1)} copy-done((f32[256,128]{1,0:T(8,128)S(1)}, f32[256,128]{1,0:T(8,128)}, u32[]{:S(2)}) %copy-start.5) | copy-done | bytes 131096
  6.9 0.0 copy-start.6
  6.9 0.7 %copy-done.6 = f32[32,128]{1,0:T(8,128)S(1)} copy-done((f32[32,128]{1,0:T(8,128)S(1)}, f32[32,128]{1,0:T(8,128)}, u32[]{:S(2)}) %copy-start.6) | copy-done | bytes 16408
  7.6 52.0 %shard_map.104 = (f32[2,256,128]{2,1,0:T(8,128)S(1)}, f32[1,16,1024]{2,1,0:T(8,128)S(1)}) custom-call(f32[256,128]{1,0:T(8,128)S(1)} %copy-done.2, f32[256,128]{1,0:T(8,128)S(1)} %copy-done.3, f32[2,256,128]{2,1,0:T(8,128)S(1)} %copy-done, f32[2,256,128]{2,1,0:T(8,128)S(1)} %copy-done.1, s32[256,128]{1,0:T(8,128)S(1)} %copy-done.4, ...), custom_call_target="tpu_custom_call" | custom-call | tf_op jit(solution)/shard_map/pallas_call | solution.py:459
  59.6 0.7 %copy.14 = f32[2,256,128]{2,1,0:T(8,128)} copy(f32[2,256,128]{2,1,0:T(8,128)S(1)} %get-tuple-element.4) | data formatting | bytes 524288
  60.3 0.6 %copy.15 = f32[1,16,1024]{2,1,0:T(8,128)} copy(f32[1,16,1024]{2,1,0:T(8,128)S(1)} %get-tuple-element.5) | data formatting | bytes 131072
Async XLA Ops:
  0.6 0.8 %copy-start.7 = (s32[64]{0:T(128)S(1)}, s32[64]{0:T(128)}, u32[]{:S(2)}) copy-start(s32[64]{0:T(128)} %owner_list.1) | copy-start | bytes 772
  1.4 1.0 %copy-start = (f32[2,256,128]{2,1,0:T(8,128)S(1)}, f32[2,256,128]{2,1,0:T(8,128)}, u32[]{:S(2)}) copy-start(f32[2,256,128]{2,1,0:T(8,128)} %drv.1) | copy-start | bytes 786436
  2.3 0.9 %copy-start.1 = (f32[2,256,128]{2,1,0:T(8,128)S(1)}, f32[2,256,128]{2,1,0:T(8,128)}, u32[]{:S(2)}) copy-start(f32[2,256,128]{2,1,0:T(8,128)} %obs.1) | copy-start | bytes 786436
  3.3 0.9 %copy-start.2 = (f32[256,128]{1,0:T(8,128)S(1)}, f32[256,128]{1,0:T(8,128)}, u32[]{:S(2)}) copy-start(f32[256,128]{1,0:T(8,128)} %visc.1) | copy-start | bytes 393220
  4.2 0.9 %copy-start.3 = (f32[256,128]{1,0:T(8,128)S(1)}, f32[256,128]{1,0:T(8,128)}, u32[]{:S(2)}) copy-start(f32[256,128]{1,0:T(8,128)} %fric.1) | copy-start | bytes 393220
  5.1 0.9 %copy-start.4 = (s32[256,128]{1,0:T(8,128)S(1)}, s32[256,128]{1,0:T(8,128)}, u32[]{:S(2)}) copy-start(s32[256,128]{1,0:T(8,128)} %mask.1) | copy-start | bytes 393220
  6.0 0.9 %copy-start.5 = (f32[256,128]{1,0:T(8,128)S(1)}, f32[256,128]{1,0:T(8,128)}, u32[]{:S(2)}) copy-start(f32[256,128]{1,0:T(8,128)} %constant.5.clone.basis_2) | copy-start | bytes 393220
  6.9 0.7 %copy-start.6 = (f32[32,128]{1,0:T(8,128)S(1)}, f32[32,128]{1,0:T(8,128)}, u32[]{:S(2)}) copy-start(f32[32,128]{1,0:T(8,128)} %constant.4.clone.basis_1) | copy-start | bytes 49156

commit v2 on v1

v2 whole, which is shorter than its diff:
```python
import functools
import math

import jax
import jax.numpy as jnp
import numpy as np
from jax import lax
from jax.experimental import pallas as pl
from jax.experimental.pallas import tpu as pltpu
from jax.sharding import PartitionSpec as P

TILE = 128
MODES = 32
LANES = 128
HALO = 8
FIELDS = 7
SWEEPS = 3
PER = LANES // MODES
SHARES = 4
LAG = 3
MESH = pl.DeviceIdType.MESH
HIGHEST = lax.Precision.HIGHEST


def bases():
    places = np.arange(TILE) + 0.5
    orders = np.arange(MODES)
    cosine = np.cos(math.pi * orders[:, None] * places[None, :] / TILE)
    first = np.concatenate([cosine[s::PER] for s in range(PER)], axis=0)
    second = np.zeros((PER * TILE, LANES))
    for s in range(PER):
        second[s * TILE : (s + 1) * TILE, s * MODES : (s + 1) * MODES] = cosine.T / TILE
    return first.astype(np.float32), second.astype(np.float32)


def around(step, size):
    return min(step % size, -step % size)


def pipeline(count, lag, *stages):
    held = {}
    for step in range(count + lag * (len(stages) - 1)):
        for i, stage in reversed(list(enumerate(stages))):
            t = step - i * lag
            if 0 <= t < count:
                held[t] = stage(t, held.pop(t, None))


def kernel(
    sizes,
    visc,
    fric,
    drv,
    obs,
    mask,
    tile_block,
    owner_list,
    basis_1,
    basis_2,
    v,
    grad,
    fm,
    mk,
    fs,
    pack,
    pack_t,
    recv_t,
    diag,
    coef,
    hb,
    w,
    w2,
    dens,
    b1,
    b2,
    tb,
    ol,
    send_a,
    recv_a,
    table,
    load_sem,
    halo_send,
    halo_recv,
    phase_send,
    phase_recv,
):
    n_row, n_own, n_col = sizes
    n_line = n_row * n_own
    rows = visc.shape[0]
    chunks = (rows + 2 * HALO) // 8
    row_at, own_at, col = (
        lax.axis_index("row"),
        lax.axis_index("own"),
        lax.axis_index("col"),
    )
    line = row_at * n_own + own_at

    def by(rows_on, owns_on, cols_on):
        return {
            "row": lax.rem(row_at + (rows_on + n_row), n_row),
            "own": lax.rem(own_at + (owns_on + n_own), n_own),
            "col": lax.rem(col + (cols_on + n_col), n_col),
        }

    def next_to(line_on, cols_on):
        to = lax.rem(line + (line_on + n_line), n_line)
        return {
            "row": lax.div(to, n_own),
            "own": lax.rem(to, n_own),
            "col": lax.rem(col + (cols_on + n_col), n_col),
        }

    col_steps = sorted(range(1, n_col), key=lambda i: -around(i, n_col))
    plane_steps = [(i, j) for i in range(n_row) for j in range(n_own) if i or j]
    plane_steps.sort(key=lambda s: -(around(s[0], n_row) + around(s[1], n_own)))

    own_rows = pl.ds(HALO, rows)
    loads = [
        (visc, fm.at[0, own_rows, :]),
        (fric, fm.at[1, own_rows, :]),
        (drv, fm.at[2:4, own_rows, :]),
        (obs, fm.at[4:6, own_rows, :]),
        (mask, mk.at[own_rows, :]),
        (basis_1, b1),
        (basis_2, b2),
        (tile_block, tb),
        (owner_list, ol),
    ]
    loads = [
        pltpu.make_async_copy(src, dst, load_sem.at[i])
        for i, (src, dst) in enumerate(loads)
    ]
    for copy in loads:
        copy.start()

    barrier = pltpu.get_barrier_semaphore()
    greeted = [next_to(i, j) for i in (-1, 1) for j in (-1, 1)]
    greeted += [by(0, 0, i) for i in reversed(col_steps)]
    greeted += [by(i, j, 0) for i, j in reversed(plane_steps)]
    for to in greeted:
        pl.semaphore_signal(barrier, inc=1, device_id=to, device_id_type=MESH)

    lane = lax.broadcasted_iota(jnp.int32, (8, LANES), 1)
    sub = lax.broadcasted_iota(jnp.int32, (8, LANES), 0)
    last_lane, first_lane, first_sub = lane == LANES - 1, lane == 0, sub == 0

    for copy in loads[:5]:
        copy.wait()

    def gather(t, _):
        at = pl.ds(HALO + 8 * t, 8)
        found = [fm[f, at, :] for f in range(6)] + [mk[at, :].astype(jnp.float32)]
        return [pltpu.roll(piece, 16 * f + 8, 1) for f, piece in enumerate(found)]

    def merge(t, pieces):
        packed = pieces[0]
        for f in range(1, FIELDS):
            packed = jnp.where(lane < 16 * f, packed, pieces[f])
        pack[8 * t : 8 * t + 8, :] = packed

    pipeline(rows // 8, 4, gather, merge)
    for part in range(rows // LANES):
        block = pack[part * LANES : (part + 1) * LANES, :]
        pack_t[:, :, part * LANES : (part + 1) * LANES] = block.T.reshape(8, 16, LANES)
    recv_t[FIELDS, :, :] = jnp.zeros((16, rows), jnp.float32)

    pl.semaphore_wait(barrier, len(greeted))
    copies = []

    def send(src, dst, to):
        at = len(copies)
        copy = pltpu.make_async_remote_copy(
            src_ref=src,
            dst_ref=dst,
            send_sem=halo_send.at[at],
            recv_sem=halo_recv.at[at],
            device_id=to,
            device_id_type=MESH,
        )
        copy.start()
        copies.append(copy)

    for line_on, source, slot in ((-1, 0, 2), (1, rows - 8, 0)):
        for cols_on in (-1, 1):
            send(
                pack.at[pl.ds(source, 8), :],
                diag.at[slot + (1 if cols_on < 0 else 0)],
                next_to(line_on, cols_on),
            )
    send(
        pack_t.at[0:FIELDS, 0:8, :], recv_t.at[0:FIELDS, 0:8, :], by(0, 0, 1)
    )
    send(
        pack_t.at[0:FIELDS, 8:16, :], recv_t.at[0:FIELDS, 8:16, :], by(0, 0, -1)
    )
    for line_on, source, target in ((-1, HALO, HALO + rows), (1, rows, 0)):
        to, take = pl.ds(target, HALO), pl.ds(source, HALO)
        send(fm.at[:, take, :], fm.at[:, to, :], next_to(line_on, 0))
        send(mk.at[take, :], mk.at[to, :], next_to(line_on, 0))

    for copy in copies:
        copy.wait_recv()

    def unpack(at, packed):
        for f in range(FIELDS):
            fs[f, at, :] = pltpu.roll(packed, LANES - (16 * f + 8), 1)

    from_left = lax.rem(lane, 16) < 8
    unpack(pl.ds(0, 8), jnp.where(from_left, diag[0], diag[1]))
    unpack(pl.ds(HALO + rows, 8), jnp.where(from_left, diag[2], diag[3]))
    for part in range(rows // LANES):
        turned = (
            recv_t[:, :, part * LANES : (part + 1) * LANES].reshape(LANES, LANES).T
        )
        for t in range(LANES // 8):
            unpack(
                pl.ds(HALO + part * LANES + 8 * t, 8), turned[8 * t : 8 * t + 8, :]
            )

    def both(fn, *args):
        return tuple(fn(*parts) for parts in zip(*args))

    def down(x, kept):
        turned = tuple(pltpu.roll(part, 1, 0) for part in x)
        moved = both(lambda k, r: jnp.where(first_sub, k, r), kept, turned)
        return moved, turned

    side_inside = ((lane < 64) & (col < n_col - 1)) | ((lane >= 64) & (col > 0))
    zero = jnp.zeros((8, LANES), jnp.float32)
    add = functools.partial(both, lambda x, y: x + y)
    sub_ = functools.partial(both, lambda x, y: x - y)

    def rolls(x, by_lanes):
        return tuple(pltpu.roll(part, by_lanes, 1) for part in x)

    def from_next(x):
        return jnp.where(last_lane, x[1], x[0]), jnp.where(last_lane, x[0], x[1])

    def from_last(x):
        return jnp.where(first_lane, x[1], x[0]), jnp.where(first_lane, x[0], x[1])

    def store_state(to, t, k, now):
        for i in range(2):
            to[i, k, 8 * t : 8 * t + 8, :] = now[i]
        return rolls(now, LANES - 1)

    def store_ahead(to, t, k, turned):
        ahead = from_next(turned)
        for i in range(2):
            to[i, 2 + k, 8 * t : 8 * t + 8, :] = ahead[i]

    def store_both_ahead(to):
        def stage(t, turned):
            for k in range(2):
                store_ahead(to, t, k, turned[k])

        return stage

    def open_(t, _):
        at = pl.ds(8 * t, 8)
        n = (fm[0, at, :], fs[0, at, :])
        inside = (None, side_inside)
        if t == 0 or t == chunks - 1:
            there = line > 0 if t == 0 else line < n_line - 1
            inside = (jnp.broadcast_to(there, (8, LANES)), side_inside & there)
            n = (jnp.where(inside[0], n[0], 0.0), n[1])
        n = (n[0], jnp.where(inside[1], n[1], 0.0))
        return n, inside, rolls(n, 1)

    summed_kept = [(zero, zero)]

    def settle(t, given):
        n, inside, turned = given
        at = pl.ds(8 * t, 8)
        ice = (mk[at, :] > 0, (fs[6, at, :] > 0.5) & inside[1])
        if inside[0] is not None:
            ice = (ice[0] & inside[0], ice[1])
        summed = add(n, from_last(turned))
        moved, summed_kept[0] = down(summed, summed_kept[0])
        states = []
        for i, source in ((0, fm), (1, fs)):
            f = source[1, at, :]
            half = jnp.where(
                ice[i], 0.5 / (1.25 * (summed[i] + moved[i]) + f), 0.0
            )
            coef[i, 0, at, :] = 0.5 * n[i]
            coef[i, 1, at, :] = 0.25 * n[i]
            coef[i, 2, at, :] = half
            coef[i, 3, at, :] = 1.0 - half * f
            scaled = [half * source[2 + k, at, :] for k in range(2)]
            for k in range(2):
                hb[i, k, at, :] = scaled[k]
            states.append([part + part for part in scaled])
        return [store_state(w, t, k, (states[0][k], states[1][k])) for k in range(2)]

    pipeline(chunks, LAG, open_, settle, store_both_ahead(w))
    for i in range(2):
        for k in range(4):
            w[i, k, 8 * chunks : 8 * chunks + 8, :] = zero
            w2[i, k, 8 * chunks : 8 * chunks + 8, :] = zero

    def turn():
        def begin(t, _):
            at = pl.ds(8 * t, 8)
            states = []
            for k in range(2):
                state = []
                for i, source in ((0, fm), (1, fs)):
                    now = w2[i, k, at, :]
                    if i == 0 and 0 < t < chunks - 1:
                        v[k, 8 * t - HALO : 8 * t - HALO + 8, :] = now
                    scaled = coef[i, 2, at, :] * (now - source[4 + k, at, :])
                    hb[i, k, at, :] = scaled
                    state.append(scaled + scaled)
                states.append(store_state(w2, t, k, tuple(state)))
            return states

        pipeline(chunks, LAG, begin, store_both_ahead(w2))

    def sweep(w_from, w_to):
        kept = [(zero, zero)] * 4

        def pull(ref, k, at):
            return ref[0, k, at, :], ref[1, k, at, :]

        def front(t, _):
            at, after = pl.ds(8 * t, 8), pl.ds(8 * t + 1, 8)
            dx, dy = [], []
            for k in range(2):
                here, here_next = pull(w_from, k, at), pull(w_from, 2 + k, at)
                below, below_next = pull(w_from, k, after), pull(w_from, 2 + k, after)
                dx.append(add(sub_(below, here), sub_(below_next, here_next)))
                dy.append(sub_(add(here_next, below_next), add(here, below)))
            m, q = pull(coef, 0, at), pull(coef, 1, at)
            total = add(dx[0], dy[1])
            product = functools.partial(both, lambda a, b: a * b)
            one = product(m, add(total, dx[0]))
            two = product(m, add(total, dy[1]))
            shear = product(q, add(dy[0], dx[1]))
            fields = (
                add(one, shear),
                sub_(one, shear),
                add(two, shear),
                sub_(shear, two),
            )
            moved = []
            for i in range(4):
                got, kept[i] = down(fields[i], kept[i])
                moved.append(got)
            stay = (sub_(moved[1], fields[0]), sub_(moved[3], fields[2]))
            go = (sub_(moved[0], fields[1]), sub_(moved[2], fields[3]))
            return stay, tuple(rolls(x, 1) for x in go)

        def close(t, given):
            at = pl.ds(8 * t, 8)
            turned = []
            for k in range(2):
                image = add(given[0][k], from_last(given[1][k]))
                now = tuple(
                    (coef[i, 3, at, :] * w_from[i, k, at, :] + hb[i, k, at, :])
                    - coef[i, 2, at, :] * image[i]
                    for i in range(2)
                )
                turned.append(store_state(w_to, t, k, now))
            return turned

        pipeline(chunks, LAG, front, close, store_both_ahead(w_to))

    def pair(s, _):
        sweep(w, w2)

        @pl.when(s == 1)
        def _():
            turn()

        sweep(w2, w)
        return 0

    lax.fori_loop(0, SWEEPS, pair, 0)

    for t in range(TILE // 8):
        total = None
        for start in range(0, rows, TILE):
            at = pl.ds(start + 8 * t, 8)
            ext = pl.ds(HALO + start + 8 * t, 8)
            piece = fm[1, ext, :] * (
                w[0, 0, ext, :] * v[0, at, :] + w[0, 1, ext, :] * v[1, at, :]
            )
            total = piece if total is None else total + piece
        dens[8 * t : 8 * t + 8, :] = -total

    for copy in loads[5:]:
        copy.wait()
    first = jnp.dot(
        b1[...], dens[...], precision=HIGHEST, preferred_element_type=jnp.float32
    )
    first = jnp.concatenate([first[8 * i : 8 * i + 8] for i in range(PER)], axis=1)
    part = jnp.dot(
        first, b2[...], precision=HIGHEST, preferred_element_type=jnp.float32
    )
    in_second = tb[0, 0] > 2 * line
    parts = jnp.where(in_second, 0.0, part), jnp.where(in_second, part, 0.0)
    per_share = 8 // SHARES
    for i in range(SHARES):
        for j in range(2):
            at = pl.ds(j * per_share, per_share)
            send_a[i, at, :] = parts[j][i * per_share : (i + 1) * per_share, :]

    def start(phase, src, dst, to):
        pltpu.make_async_remote_copy(
            src_ref=src,
            dst_ref=dst,
            send_sem=phase_send.at[phase],
            recv_sem=phase_recv.at[phase],
            device_id=to,
            device_id_type=MESH,
        ).start()

    def arrived(phase, ref):
        pltpu.make_async_copy(ref, ref, phase_recv.at[phase]).wait()

    def departed(phase, ref):
        pltpu.make_async_copy(ref, ref, phase_send.at[phase]).wait()

    share = lax.rem(col, SHARES)
    for i in col_steps:
        to = by(0, 0, i)
        start(0, send_a.at[lax.rem(to["col"], SHARES)], recv_a.at[col], to)
    recv_a[col] = send_a[share]
    arrived(0, recv_a.at[0 : n_col - 1])
    total = recv_a[0]
    for i in range(1, n_col):
        total = total + recv_a[i]

    mine = table.at[pl.ds(2 * line, 2)]
    for j in range(2):
        table[2 * line + j] = total[j * per_share : (j + 1) * per_share, :]
    for i, j in plane_steps:
        start(1, mine, mine, by(i, j, 0))
    arrived(1, table.at[0 : 2 * n_line - 2])

    per_owner = ol.shape[0] // n_own
    width = per_share * LANES
    for k in range(per_owner):
        entry = table[ol[own_at * per_owner + k]]
        for j in range(per_share):
            at = pl.ds(pl.multiple_of(share * width + j * LANES, LANES), LANES)
            grad[0, k : k + 1, at] = entry[j : j + 1, :]

    mine_c = grad.at[0, :, pl.ds(pl.multiple_of(share * width, LANES), width)]
    for i in range(1, SHARES):
        to = {"row": row_at, "own": own_at, "col": lax.bitwise_xor(col, i)}
        start(2, mine_c, mine_c, to)
    arrived(2, grad.at[0, :, 0 : (SHARES - 1) * width])

    for copy in copies:
        copy.wait_send()
    departed(0, recv_a.at[0 : n_col - 1])
    departed(1, table.at[0 : 2 * n_line - 2])
    departed(2, grad.at[0, :, 0 : (SHARES - 1) * width])


def solution(mesh):
    sizes = tuple(mesh.shape[a] for a in ("row", "own", "col"))
    n_line, n_col = sizes[0] * sizes[1], sizes[2]

    def local(viscosity, friction, driving, observed, ice_mask, tile_block, owner_list):
        rows = viscosity.shape[0]
        ext = rows + 2 * HALO
        first, second = bases()
        per_owner = owner_list.shape[0] // sizes[1]
        f32 = jnp.float32
        vmem = pltpu.VMEM
        tile_block = tile_block.reshape(1, -1)
        operands = (
            viscosity,
            friction,
            driving,
            observed,
            ice_mask,
            tile_block,
            owner_list,
            jnp.asarray(first),
            jnp.asarray(second),
        )
        return pl.pallas_call(
            functools.partial(kernel, sizes),
            out_shape=(
                jax.ShapeDtypeStruct((2, rows, LANES), f32),
                jax.ShapeDtypeStruct((1, per_owner, MODES * MODES), f32),
            ),
            in_specs=[pl.BlockSpec(memory_space=pltpu.HBM)] * 9,
            out_specs=[pl.BlockSpec(memory_space=pltpu.VMEM)] * 2,
            scratch_shapes=[
                vmem((6, ext, LANES), f32),
                vmem((ext, LANES), jnp.int32),
                vmem((FIELDS, ext, LANES), f32),
                vmem((rows, LANES), f32),
                vmem((8, 16, rows), f32),
                vmem((8, 16, rows), f32),
                vmem((4, 8, LANES), f32),
                vmem((2, 4, ext, LANES), f32),
                vmem((2, 2, ext, LANES), f32),
                vmem((2, 4, ext + 8, LANES), f32),
                vmem((2, 4, ext + 8, LANES), f32),
                vmem((TILE, LANES), f32),
                vmem(first.shape, f32),
                vmem(second.shape, f32),
                pltpu.SMEM(tile_block.shape, jnp.int32),
                pltpu.SMEM(owner_list.shape, jnp.int32),
                vmem((SHARES, 2 * 8 // SHARES, LANES), f32),
                vmem((n_col, 2 * 8 // SHARES, LANES), f32),
                vmem((2 * n_line, 8 // SHARES, LANES), f32),
                pltpu.SemaphoreType.DMA((9,)),
                pltpu.SemaphoreType.DMA((10,)),
                pltpu.SemaphoreType.DMA((10,)),
                pltpu.SemaphoreType.DMA((3,)),
                pltpu.SemaphoreType.DMA((3,)),
            ],
            compiler_params=pltpu.CompilerParams(
                collective_id=0,
                has_side_effects=True,
                vmem_limit_bytes=32 * 2**20,
            ),
        )(*(pltpu.with_memory_space_constraint(x, pltpu.HBM) for x in operands))

    return jax.shard_map(
        local,
        mesh=mesh,
        in_specs=(
            P(("row", "own"), "col"),
            P(("row", "own"), "col"),
            P(None, ("row", "own"), "col"),
            P(None, ("row", "own"), "col"),
            P(("row", "own"), "col"),
            P(("row", "own"), "col"),
            P(),
        ),
        out_specs=(P(None, ("row", "own"), "col"), P("own", None, None)),
        check_vma=False,
    )
```

time: 61.3 us -> 42.5 us (0.69)
  Pallas kernels: 52 us -> 40.3 us
  local copies, waits for them, and re-layouts: 8.32 us -> 1.33 us
    pallas_call x1, Pallas kernels: 52 us -> 40.3 us  [local(): pl.pallas_call(functools.partial(kernel, sizes), out_shape=(jax.ShapeDtyp...]
    unnamed x19 -> x2, local copies, waits for them, and re-layouts: 8.32 us -> 1.33 us
where the time goes in v2:
time: 42.5 us; the launch traced here: 42.3 us
  Pallas kernels  40.3 us (95%)
  local copies, waits for them, and re-layouts  1.33 us (3%)
  between operations  0.64 us (2%)
    pallas_call x1, Pallas kernels, local(): pl.pallas_call(functools.partial(kernel, sizes), out_shape=(jax.ShapeDtyp...  40.3 us
    unnamed x2, local copies, waits for them, and re-layouts  1.33 us

profile of v2, /device:TPU:1, one launch (start us, length us, event | category | flops | bytes accessed | tf_op | source)
XLA Modules:
  0.0 42.3 jit_solution(15044791243689355004)
XLA Ops:
  0.6 40.3 %shard_map.104 = (f32[2,256,128]{2,1,0:T(8,128)S(1)}, f32[1,16,1024]{2,1,0:T(8,128)S(1)}) custom-call(f32[256,128]{1,0:T(8,128)} %visc.1, f32[256,128]{1,0:T(8,128)} %fric.1, f32[2,256,128]{2,1,0:T(8,128)} %drv.1, f32[2,256,128]{2,1,0:T(8,128)} %obs.1, s32[256,128]{1,0:T(8,128)} %mask.1, s32[1,2]{1,0:T(1,128)} %bitcast.1, s32[64]{0:T(128)} %owner_list.1, ...), custom_call_target="tpu_custom_call" | custom-call | tf_op jit(solution)/shard_map/pallas_call | solution.py:486
  41.0 0.7 %copy.13 = f32[2,256,128]{2,1,0:T(8,128)} copy(f32[2,256,128]{2,1,0:T(8,128)S(1)} %get-tuple-element.4) | data formatting | bytes 524288
  41.7 0.6 %copy.14 = f32[1,16,1024]{2,1,0:T(8,128)} copy(f32[1,16,1024]{2,1,0:T(8,128)S(1)} %get-tuple-element.5) | data formatting | bytes 131072

commit v3 on v2

--- a/solution.py
+++ b/solution.py
@@ -17,7 +17,7 @@
 SWEEPS = 3
 PER = LANES // MODES
 SHARES = 4
-LAG = 3
+LAG = 8
 MESH = pl.DeviceIdType.MESH
 HIGHEST = lax.Precision.HIGHEST
 
@@ -46,26 +46,142 @@
                 held[t] = stage(t, held.pop(t, None))
 
 
-def kernel(
+def exchange(
     sizes,
     visc,
     fric,
     drv,
     obs,
     mask,
+    fm,
+    mk,
+    recv_t,
+    diag,
+    pack,
+    pack_t,
+    load_sem,
+    halo_send,
+    halo_recv,
+):
+    n_row, n_own, n_col = sizes
+    n_line = n_row * n_own
+    rows = visc.shape[0]
+    row_at, own_at, col = (
+        lax.axis_index("row"),
+        lax.axis_index("own"),
+        lax.axis_index("col"),
+    )
+    line = row_at * n_own + own_at
+
+    def by(rows_on, owns_on, cols_on):
+        return {
+            "row": lax.rem(row_at + (rows_on + n_row), n_row),
+            "own": lax.rem(own_at + (owns_on + n_own), n_own),
+            "col": lax.rem(col + (cols_on + n_col), n_col),
+        }
+
+    def next_to(line_on, cols_on):
+        to = lax.rem(line + (line_on + n_line), n_line)
+        return {
+            "row": lax.div(to, n_own),
+            "own": lax.rem(to, n_own),
+            "col": lax.rem(col + (cols_on + n_col), n_col),
+        }
+
+    own_rows = pl.ds(HALO, rows)
+    loads = [
+        (visc, fm.at[0, own_rows, :]),
+        (fric, fm.at[1, own_rows, :]),
+        (drv, fm.at[2:4, own_rows, :]),
+        (obs, fm.at[4:6, own_rows, :]),
+        (mask, mk.at[own_rows, :]),
+    ]
+    loads = [
+        pltpu.make_async_copy(src, dst, load_sem.at[i])
+        for i, (src, dst) in enumerate(loads)
+    ]
+    for copy in loads:
+        copy.start()
+
+    barrier = pltpu.get_barrier_semaphore()
+    greeted = [next_to(i, j) for i in (-1, 1) for j in (-1, 0, 1)]
+    greeted += [by(0, 0, i) for i in (-1, 1)]
+    for to in greeted:
+        pl.semaphore_signal(barrier, inc=1, device_id=to, device_id_type=MESH)
+
+    lane = lax.broadcasted_iota(jnp.int32, (8, LANES), 1)
+
+    for copy in loads:
+        copy.wait()
+
+    def gather(t, _):
+        at = pl.ds(HALO + 8 * t, 8)
+        found = [fm[f, at, :] for f in range(6)] + [mk[at, :].astype(jnp.float32)]
+        return [pltpu.roll(piece, 16 * f + 8, 1) for f, piece in enumerate(found)]
+
+    def merge(t, pieces):
+        packed = pieces[0]
+        for f in range(1, FIELDS):
+            packed = jnp.where(lane < 16 * f, packed, pieces[f])
+        pack[8 * t : 8 * t + 8, :] = packed
+
+    pipeline(rows // 8, 4, gather, merge)
+    for part in range(rows // LANES):
+        block = pack[part * LANES : (part + 1) * LANES, :]
+        pack_t[:, :, part * LANES : (part + 1) * LANES] = block.T.reshape(8, 16, LANES)
+    recv_t[FIELDS, :, :] = jnp.zeros((16, rows), jnp.float32)
+
+    pl.semaphore_wait(barrier, len(greeted))
+    copies = []
+
+    def send(src, dst, to):
+        at = len(copies)
+        copy = pltpu.make_async_remote_copy(
+            src_ref=src,
+            dst_ref=dst,
+            send_sem=halo_send.at[at],
+            recv_sem=halo_recv.at[at],
+            device_id=to,
+            device_id_type=MESH,
+        )
+        copy.start()
+        copies.append(copy)
+
+    for line_on, source, slot in ((-1, 0, 2), (1, rows - 8, 0)):
+        for cols_on in (-1, 1):
+            send(
+                pack.at[pl.ds(source, 8), :],
+                diag.at[slot + (1 if cols_on < 0 else 0)],
+                next_to(line_on, cols_on),
+            )
+    send(
+        pack_t.at[0:FIELDS, 0:8, :], recv_t.at[0:FIELDS, 0:8, :], by(0, 0, 1)
+    )
+    send(
+        pack_t.at[0:FIELDS, 8:16, :], recv_t.at[0:FIELDS, 8:16, :], by(0, 0, -1)
+    )
+    for line_on, source, target in ((-1, HALO, HALO + rows), (1, rows, 0)):
+        to, take = pl.ds(target, HALO), pl.ds(source, HALO)
+        send(fm.at[:, take, :], fm.at[:, to, :], next_to(line_on, 0))
+        send(mk.at[take, :], mk.at[to, :], next_to(line_on, 0))
+
+    for copy in copies:
+        copy.wait()
+
+
+def kernel(
+    sizes,
+    fm,
+    mk,
+    recv_t,
+    diag,
     tile_block,
     owner_list,
     basis_1,
     basis_2,
     v,
     grad,
-    fm,
-    mk,
     fs,
-    pack,
-    pack_t,
-    recv_t,
-    diag,
     coef,
     hb,
     w,
@@ -79,14 +195,12 @@
     recv_a,
     table,
     load_sem,
-    halo_send,
-    halo_recv,
     phase_send,
     phase_recv,
 ):
     n_row, n_own, n_col = sizes
     n_line = n_row * n_own
-    rows = visc.shape[0]
+    rows = fm.shape[1] - 2 * HALO
     chunks = (rows + 2 * HALO) // 8
     row_at, own_at, col = (
         lax.axis_index("row"),
@@ -102,25 +216,11 @@
             "col": lax.rem(col + (cols_on + n_col), n_col),
         }
 
-    def next_to(line_on, cols_on):
-        to = lax.rem(line + (line_on + n_line), n_line)
-        return {
-            "row": lax.div(to, n_own),
-            "own": lax.rem(to, n_own),
-            "col": lax.rem(col + (cols_on + n_col), n_col),
-        }
-
     col_steps = sorted(range(1, n_col), key=lambda i: -around(i, n_col))
     plane_steps = [(i, j) for i in range(n_row) for j in range(n_own) if i or j]
     plane_steps.sort(key=lambda s: -(around(s[0], n_row) + around(s[1], n_own)))
 
-    own_rows = pl.ds(HALO, rows)
     loads = [
-        (visc, fm.at[0, own_rows, :]),
-        (fric, fm.at[1, own_rows, :]),
-        (drv, fm.at[2:4, own_rows, :]),
-        (obs, fm.at[4:6, own_rows, :]),
-        (mask, mk.at[own_rows, :]),
         (basis_1, b1),
         (basis_2, b2),
         (tile_block, tb),
@@ -134,72 +234,14 @@
         copy.start()
 
     barrier = pltpu.get_barrier_semaphore()
-    greeted = [next_to(i, j) for i in (-1, 1) for j in (-1, 1)]
-    greeted += [by(0, 0, i) for i in reversed(col_steps)]
-    greeted += [by(i, j, 0) for i, j in reversed(plane_steps)]
+    greeted = [by(0, 0, i) for i in col_steps]
+    greeted += [by(i, j, 0) for i, j in plane_steps]
     for to in greeted:
         pl.semaphore_signal(barrier, inc=1, device_id=to, device_id_type=MESH)
 
     lane = lax.broadcasted_iota(jnp.int32, (8, LANES), 1)
     sub = lax.broadcasted_iota(jnp.int32, (8, LANES), 0)
     last_lane, first_lane, first_sub = lane == LANES - 1, lane == 0, sub == 0
-
-    for copy in loads[:5]:
-        copy.wait()
-
-    def gather(t, _):
-        at = pl.ds(HALO + 8 * t, 8)
-        found = [fm[f, at, :] for f in range(6)] + [mk[at, :].astype(jnp.float32)]
-        return [pltpu.roll(piece, 16 * f + 8, 1) for f, piece in enumerate(found)]
-
-    def merge(t, pieces):
-        packed = pieces[0]
-        for f in range(1, FIELDS):
-            packed = jnp.where(lane < 16 * f, packed, pieces[f])
-        pack[8 * t : 8 * t + 8, :] = packed
-
-    pipeline(rows // 8, 4, gather, merge)
-    for part in range(rows // LANES):
-        block = pack[part * LANES : (part + 1) * LANES, :]
-        pack_t[:, :, part * LANES : (part + 1) * LANES] = block.T.reshape(8, 16, LANES)
-    recv_t[FIELDS, :, :] = jnp.zeros((16, rows), jnp.float32)
-
-    pl.semaphore_wait(barrier, len(greeted))
-    copies = []
-
-    def send(src, dst, to):
-        at = len(copies)
-        copy = pltpu.make_async_remote_copy(
-            src_ref=src,
-            dst_ref=dst,
-            send_sem=halo_send.at[at],
-            recv_sem=halo_recv.at[at],
-            device_id=to,
-            device_id_type=MESH,
-        )
-        copy.start()
-        copies.append(copy)
-
-    for line_on, source, slot in ((-1, 0, 2), (1, rows - 8, 0)):
-        for cols_on in (-1, 1):
-            send(
-                pack.at[pl.ds(source, 8), :],
-                diag.at[slot + (1 if cols_on < 0 else 0)],
-                next_to(line_on, cols_on),
-            )
-    send(
-        pack_t.at[0:FIELDS, 0:8, :], recv_t.at[0:FIELDS, 0:8, :], by(0, 0, 1)
-    )
-    send(
-        pack_t.at[0:FIELDS, 8:16, :], recv_t.at[0:FIELDS, 8:16, :], by(0, 0, -1)
-    )
-    for line_on, source, target in ((-1, HALO, HALO + rows), (1, rows, 0)):
-        to, take = pl.ds(target, HALO), pl.ds(source, HALO)
-        send(fm.at[:, take, :], fm.at[:, to, :], next_to(line_on, 0))
-        send(mk.at[take, :], mk.at[to, :], next_to(line_on, 0))
-
-    for copy in copies:
-        copy.wait_recv()
 
     def unpack(at, packed):
         for f in range(FIELDS):
@@ -389,7 +431,7 @@
             total = piece if total is None else total + piece
         dens[8 * t : 8 * t + 8, :] = -total
 
-    for copy in loads[5:]:
+    for copy in loads:
         copy.wait()
     first = jnp.dot(
         b1[...], dens[...], precision=HIGHEST, preferred_element_type=jnp.float32
@@ -422,6 +464,7 @@
     def departed(phase, ref):
         pltpu.make_async_copy(ref, ref, phase_send.at[phase]).wait()
 
+    pl.semaphore_wait(barrier, len(greeted))
     share = lax.rem(col, SHARES)
     for i in col_steps:
         to = by(0, 0, i)
@@ -453,8 +496,6 @@
         start(2, mine_c, mine_c, to)
     arrived(2, grad.at[0, :, 0 : (SHARES - 1) * width])
 
-    for copy in copies:
-        copy.wait_send()
     departed(0, recv_a.at[0 : n_col - 1])
     departed(1, table.at[0 : 2 * n_line - 2])
     departed(2, grad.at[0, :, 0 : (SHARES - 1) * width])
@@ -471,34 +512,49 @@
         per_owner = owner_list.shape[0] // sizes[1]
         f32 = jnp.float32
         vmem = pltpu.VMEM
+        fields = (viscosity, friction, driving, observed, ice_mask)
         tile_block = tile_block.reshape(1, -1)
-        operands = (
-            viscosity,
-            friction,
-            driving,
-            observed,
-            ice_mask,
-            tile_block,
-            owner_list,
-            jnp.asarray(first),
-            jnp.asarray(second),
-        )
+        small = (tile_block, owner_list, jnp.asarray(first), jnp.asarray(second))
+        hbm = pl.BlockSpec(memory_space=pltpu.HBM)
+        here = pl.BlockSpec(memory_space=pltpu.VMEM)
+        dma = pltpu.SemaphoreType.DMA
+
+        def pinned(operands):
+            return [pltpu.with_memory_space_constraint(x, pltpu.HBM) for x in operands]
+
+        padded = pl.pallas_call(
+            functools.partial(exchange, sizes),
+            out_shape=(
+                jax.ShapeDtypeStruct((6, ext, LANES), f32),
+                jax.ShapeDtypeStruct((ext, LANES), jnp.int32),
+                jax.ShapeDtypeStruct((8, 16, rows), f32),
+                jax.ShapeDtypeStruct((4, 8, LANES), f32),
+            ),
+            in_specs=[hbm] * 5,
+            out_specs=[here] * 4,
+            scratch_shapes=[
+                vmem((rows, LANES), f32),
+                vmem((8, 16, rows), f32),
+                dma((5,)),
+                dma((10,)),
+                dma((10,)),
+            ],
+            compiler_params=pltpu.CompilerParams(
+                collective_id=0,
+                has_side_effects=True,
+                vmem_limit_bytes=16 * 2**20,
+            ),
+        )(*pinned(fields))
         return pl.pallas_call(
             functools.partial(kernel, sizes),
             out_shape=(
                 jax.ShapeDtypeStruct((2, rows, LANES), f32),
                 jax.ShapeDtypeStruct((1, per_owner, MODES * MODES), f32),
             ),
-            in_specs=[pl.BlockSpec(memory_space=pltpu.HBM)] * 9,
-            out_specs=[pl.BlockSpec(memory_space=pltpu.VMEM)] * 2,
+            in_specs=[here] * 4 + [hbm] * 4,
+            out_specs=[here] * 2,
             scratch_shapes=[
-                vmem((6, ext, LANES), f32),
-                vmem((ext, LANES), jnp.int32),
                 vmem((FIELDS, ext, LANES), f32),
-                vmem((rows, LANES), f32),
-                vmem((8, 16, rows), f32),
-                vmem((8, 16, rows), f32),
-                vmem((4, 8, LANES), f32),
                 vmem((2, 4, ext, LANES), f32),
                 vmem((2, 2, ext, LANES), f32),
                 vmem((2, 4, ext + 8, LANES), f32),
@@ -511,18 +567,16 @@
                 vmem((SHARES, 2 * 8 // SHARES, LANES), f32),
                 vmem((n_col, 2 * 8 // SHARES, LANES), f32),
                 vmem((2 * n_line, 8 // SHARES, LANES), f32),
-                pltpu.SemaphoreType.DMA((9,)),
-                pltpu.SemaphoreType.DMA((10,)),
-                pltpu.SemaphoreType.DMA((10,)),
-                pltpu.SemaphoreType.DMA((3,)),
-                pltpu.SemaphoreType.DMA((3,)),
+                dma((4,)),
+                dma((3,)),
+                dma((3,)),
             ],
             compiler_params=pltpu.CompilerParams(
-                collective_id=0,
+                collective_id=1,
                 has_side_effects=True,
                 vmem_limit_bytes=32 * 2**20,
             ),
-        )(*(pltpu.with_memory_space_constraint(x, pltpu.HBM) for x in operands))
+        )(*padded, *pinned(small))
 
     return jax.shard_map(
         local,

time: 42.5 us -> 40.5 us (0.953)
  Pallas kernels: 40.3 us -> 38.4 us
    pallas_call x1, Pallas kernels: 40.3 us -> 20.2 us  [local(): pl.pallas_call(functools.partial(kernel, sizes), out_shape=(jax.ShapeDtyp...]
    pallas_call x0 -> x1, Pallas kernels: none -> 18.2 us  [local(): pl.pallas_call(functools.partial(exchange, sizes), out_shape=(jax.ShapeDt...]
where the time goes in v3:
time: 40.5 us; the launch traced here: 40.4 us
  Pallas kernels  38.4 us (95%)
  local copies, waits for them, and re-layouts  1.33 us (3%)
  between operations  0.65 us (2%)
    pallas_call x1, Pallas kernels, local(): pl.pallas_call(functools.partial(kernel, sizes), out_shape=(jax.ShapeDtyp...  20.2 us
    pallas_call x1, Pallas kernels, local(): pl.pallas_call(functools.partial(exchange, sizes), out_shape=(jax.ShapeDt...  18.2 us
    unnamed x2, local copies, waits for them, and re-layouts  1.33 us

profile of v3, /device:TPU:1, one launch (start us, length us, event | category | flops | bytes accessed | tf_op | source)
XLA Modules:
  0.0 40.4 jit_solution(13903919394294086414)
XLA Ops:
  0.6 18.2 %shard_map.104 = (f32[6,272,128]{2,1,0:T(8,128)S(1)}, s32[272,128]{1,0:T(8,128)S(1)}, f32[8,16,256]{2,1,0:T(8,128)S(1)}, f32[4,8,128]{2,1,0:T(8,128)S(1)}) custom-call(f32[256,128]{1,0:T(8,128)} %visc.1, f32[256,128]{1,0:T(8,128)} %fric.1, f32[2,256,128]{2,1,0:T(8,128)} %drv.1, f32[2,256,128]{2,1,0:T(8,128)} %obs.1, s32[256,128]{1,0:T(8,128)} %mask.1), custom_call_target="tpu_custom_call" | custom-call | tf_op jit(solution)/shard_map/pallas_call | solution.py:525
  18.8 20.2 %shard_map.105 = (f32[2,256,128]{2,1,0:T(8,128)S(1)}, f32[1,16,1024]{2,1,0:T(8,128)S(1)}) custom-call(f32[6,272,128]{2,1,0:T(8,128)S(1)} %get-tuple-element.6.fm, s32[272,128]{1,0:T(8,128)S(1)} %get-tuple-element.7.mk, f32[8,16,256]{2,1,0:T(8,128)S(1)} %get-tuple-element.8.recv_t, f32[4,8,128]{2,1,0:T(8,128)S(1)} %get-tuple-element.9.diag, s32[1,2]{1,0:T(1,128)} %bitcast.1, ...), custom_call_target="tpu_custom_call" | custom-call | tf_op jit(solution)/shard_map/pallas_call | solution.py:548
  39.0 0.7 %copy.13 = f32[2,256,128]{2,1,0:T(8,128)} copy(f32[2,256,128]{2,1,0:T(8,128)S(1)} %get-tuple-element.12) | data formatting | bytes 524288
  39.7 0.6 %copy.14 = f32[1,16,1024]{2,1,0:T(8,128)} copy(f32[1,16,1024]{2,1,0:T(8,128)S(1)} %get-tuple-element.13) | data formatting | bytes 131072

commit v4 on v3

--- a/solution.py
+++ b/solution.py
@@ -17,7 +17,7 @@
 SWEEPS = 3
 PER = LANES // MODES
 SHARES = 4
-LAG = 8
+LAG = 12
 MESH = pl.DeviceIdType.MESH
 HIGHEST = lax.Precision.HIGHEST
 
@@ -44,6 +44,123 @@
             t = step - i * lag
             if 0 <= t < count:
                 held[t] = stage(t, held.pop(t, None))
+
+
+def solve(chunks, refs, n_of, ice_of, field, keep):
+    coef, hb, w, w2 = refs
+    first_sub = lax.broadcasted_iota(jnp.int32, (8, LANES), 0) == 0
+    zero = jnp.zeros((8, LANES), jnp.float32)
+
+    def rows_of(t):
+        return slice(8 * t, 8 * t + 8)
+
+    def down(x, kept):
+        turned = pltpu.roll(x, 1, 0)
+        return jnp.where(first_sub, kept, turned), turned
+
+    def store_state(to, t, k, now):
+        to[k, rows_of(t), :] = now
+        return pltpu.roll(now, LANES - 1, 1)
+
+    def store_ahead(to):
+        def stage(t, turned):
+            for k in range(2):
+                to[2 + k, rows_of(t), :] = turned[k]
+
+        return stage
+
+    def open_(t, _):
+        n = n_of(t)
+        return n, pltpu.roll(n, 1, 1)
+
+    summed_kept = [zero]
+
+    def settle(t, given):
+        n, turned = given
+        at = rows_of(t)
+        summed = n + turned
+        moved, summed_kept[0] = down(summed, summed_kept[0])
+        f = field(1, t)
+        half = jnp.where(ice_of(t), 0.5 / (1.25 * (summed + moved) + f), 0.0)
+        coef[0, at, :] = 0.5 * n
+        coef[1, at, :] = 0.25 * n
+        coef[2, at, :] = half
+        coef[3, at, :] = 1.0 - half * f
+        out = []
+        for k in range(2):
+            scaled = half * field(2 + k, t)
+            hb[k, at, :] = scaled
+            out.append(store_state(w, t, k, scaled + scaled))
+        return out
+
+    pipeline(chunks, LAG, open_, settle, store_ahead(w))
+    for k in range(4):
+        w[k, rows_of(chunks), :] = zero
+        w2[k, rows_of(chunks), :] = zero
+
+    def turn():
+        def begin(t, _):
+            at = rows_of(t)
+            out = []
+            for k in range(2):
+                now = w2[k, at, :]
+                keep(t, k, now)
+                scaled = coef[2, at, :] * (now - field(4 + k, t))
+                hb[k, at, :] = scaled
+                out.append(store_state(w2, t, k, scaled + scaled))
+            return out
+
+        pipeline(chunks, LAG, begin, store_ahead(w2))
+
+    def sweep(w_from, w_to):
+        kept = [zero] * 4
+
+        def front(t, _):
+            at, after = rows_of(t), slice(8 * t + 1, 8 * t + 9)
+            dx, dy = [], []
+            for k in range(2):
+                here, here_next = w_from[k, at, :], w_from[2 + k, at, :]
+                below, below_next = w_from[k, after, :], w_from[2 + k, after, :]
+                dx.append((below - here) + (below_next - here_next))
+                dy.append((here_next + below_next) - (here + below))
+            m, q = coef[0, at, :], coef[1, at, :]
+            total = dx[0] + dy[1]
+            one = m * (total + dx[0])
+            two = m * (total + dy[1])
+            shear = q * (dy[0] + dx[1])
+            fields = (one + shear, one - shear, two + shear, shear - two)
+            moved = []
+            for i in range(4):
+                got, kept[i] = down(fields[i], kept[i])
+                moved.append(got)
+            stay = (moved[1] - fields[0], moved[3] - fields[2])
+            go = (moved[0] - fields[1], moved[2] - fields[3])
+            return stay, tuple(pltpu.roll(x, 1, 1) for x in go)
+
+        def close(t, given):
+            at = rows_of(t)
+            turned = []
+            for k in range(2):
+                image = given[0][k] + given[1][k]
+                now = (
+                    coef[3, at, :] * w_from[k, at, :] + hb[k, at, :]
+                ) - coef[2, at, :] * image
+                turned.append(store_state(w_to, t, k, now))
+            return turned
+
+        pipeline(chunks, LAG, front, close, store_ahead(w_to))
+
+    def pair(s, _):
+        sweep(w, w2)
+
+        @pl.when(s == 1)
+        def _():
+            turn()
+
+        sweep(w2, w)
+        return 0
+
+    lax.fori_loop(0, SWEEPS, pair, 0)
 
 
 def exchange(
@@ -57,8 +174,15 @@
     mk,
     recv_t,
     diag,
+    beside,
+    v,
+    dm,
     pack,
     pack_t,
+    coef,
+    hb,
+    w,
+    w2,
     load_sem,
     halo_send,
     halo_recv,
@@ -129,7 +253,7 @@
     for part in range(rows // LANES):
         block = pack[part * LANES : (part + 1) * LANES, :]
         pack_t[:, :, part * LANES : (part + 1) * LANES] = block.T.reshape(8, 16, LANES)
-    recv_t[FIELDS, :, :] = jnp.zeros((16, rows), jnp.float32)
+    recv_t[FIELDS : 16 - FIELDS] = jnp.zeros((2, 8, rows), jnp.float32)
 
     pl.semaphore_wait(barrier, len(greeted))
     copies = []
@@ -154,16 +278,43 @@
                 diag.at[slot + (1 if cols_on < 0 else 0)],
                 next_to(line_on, cols_on),
             )
-    send(
-        pack_t.at[0:FIELDS, 0:8, :], recv_t.at[0:FIELDS, 0:8, :], by(0, 0, 1)
-    )
-    send(
-        pack_t.at[0:FIELDS, 8:16, :], recv_t.at[0:FIELDS, 8:16, :], by(0, 0, -1)
-    )
+    send(pack_t.at[0:FIELDS, 0:8, :], recv_t.at[0:FIELDS], by(0, 0, 1))
+    send(pack_t.at[0:FIELDS, 8:16, :], recv_t.at[16 - FIELDS : 16], by(0, 0, -1))
     for line_on, source, target in ((-1, HALO, HALO + rows), (1, rows, 0)):
         to, take = pl.ds(target, HALO), pl.ds(source, HALO)
         send(fm.at[:, take, :], fm.at[:, to, :], next_to(line_on, 0))
         send(mk.at[take, :], mk.at[to, :], next_to(line_on, 0))
+
+    def turn_half(t, _):
+        at = pl.ds(HALO + 8 * t, 8)
+        found = [fm[f, at, :] for f in range(6)] + [mk[at, :].astype(jnp.float32)]
+        return [(x, pltpu.roll(x, 64, 1)) for x in found]
+
+    def put_half(t, pieces):
+        for f, (x, turned) in enumerate(pieces):
+            beside[f, 8 * t : 8 * t + 8, :] = jnp.where(lane < 32, x, turned)
+
+    pipeline(rows // 8, 2, turn_half, put_half)
+
+    def field(f, t):
+        return fm[f, HALO + 8 * t : HALO + 8 * t + 8, :]
+
+    def keep(t, k, now):
+        v[k, 8 * t : 8 * t + 8, :] = now
+
+    solve(
+        rows // 8,
+        (coef, hb, w, w2),
+        lambda t: field(0, t),
+        lambda t: mk[HALO + 8 * t : HALO + 8 * t + 8, :] > 0,
+        field,
+        keep,
+    )
+    for t in range(1, rows // 8 - 1):
+        at = slice(8 * t, 8 * t + 8)
+        dm[at, :] = field(1, t) * (
+            w[0, at, :] * v[0, at, :] + w[1, at, :] * v[1, at, :]
+        )
 
     for copy in copies:
         copy.wait()
@@ -175,6 +326,9 @@
     mk,
     recv_t,
     diag,
+    beside,
+    v_in,
+    dm,
     tile_block,
     owner_list,
     basis_1,
@@ -186,6 +340,7 @@
     hb,
     w,
     w2,
+    vx,
     dens,
     b1,
     b2,
@@ -240,196 +395,106 @@
         pl.semaphore_signal(barrier, inc=1, device_id=to, device_id_type=MESH)
 
     lane = lax.broadcasted_iota(jnp.int32, (8, LANES), 1)
-    sub = lax.broadcasted_iota(jnp.int32, (8, LANES), 0)
-    last_lane, first_lane, first_sub = lane == LANES - 1, lane == 0, sub == 0
-
-    def unpack(at, packed):
+
+    def corners(e, left, right):
+        at = pl.ds(8 * e, 8)
         for f in range(FIELDS):
-            fs[f, at, :] = pltpu.roll(packed, LANES - (16 * f + 8), 1)
-
-    from_left = lax.rem(lane, 16) < 8
-    unpack(pl.ds(0, 8), jnp.where(from_left, diag[0], diag[1]))
-    unpack(pl.ds(HALO + rows, 8), jnp.where(from_left, diag[2], diag[3]))
-    for part in range(rows // LANES):
-        turned = (
-            recv_t[:, :, part * LANES : (part + 1) * LANES].reshape(LANES, LANES).T
+            x = fm[f, at, :] if f < 6 else mk[at, :].astype(jnp.float32)
+            own = jnp.where(lane < 32, x, pltpu.roll(x, 64, 1))
+            far = jnp.where(
+                lane < 96,
+                pltpu.roll(right, (56 - 16 * f) % LANES, 1),
+                pltpu.roll(left, (120 - 16 * f) % LANES, 1),
+            )
+            fs[f, at, :] = jnp.where(lane < 64, own, far)
+
+    corners(0, diag[0], diag[1])
+    corners(chunks - 1, diag[2], diag[3])
+    blocks = [
+        recv_t[:, :, part * LANES : (part + 1) * LANES].reshape(LANES, LANES).T
+        for part in range(rows // LANES)
+    ]
+
+    def spread(t, _):
+        packed = blocks[8 * t // LANES][8 * t % LANES : 8 * t % LANES + 8, :]
+        return [pltpu.roll(packed, (120 - 8 * f) % LANES, 1) for f in range(FIELDS)]
+
+    def put(t, turned):
+        at = slice(8 * t, 8 * t + 8)
+        for f in range(FIELDS):
+            fs[f, HALO + 8 * t : HALO + 8 * t + 8, :] = jnp.where(
+                lane < 64, beside[f, at, :], turned[f]
+            )
+
+    pipeline(rows // 8, 4, spread, put)
+
+    ends = [0, 1, 2, chunks - 3, chunks - 2, chunks - 1]
+    upper, lower, strips = 1, 4, len(ends)
+
+    def place(t):
+        return (fm, ends[t]) if t < strips else (fs, t - strips)
+
+    def field(f, t):
+        source, e = place(t)
+        return source[f, 8 * e : 8 * e + 8, :]
+
+    strip_inside = (
+        (lane < 64)
+        | ((lane < 96) & (col < n_col - 1))
+        | ((lane >= 96) & (col > 0))
+    )
+
+    def inside(t):
+        e = place(t)[1]
+        mask = strip_inside if t >= strips else None
+        if e == 0 or e == chunks - 1:
+            there = jnp.broadcast_to(
+                line > 0 if e == 0 else line < n_line - 1, (8, LANES)
+            )
+            mask = there if mask is None else mask & there
+        return mask
+
+    def n_of(t):
+        mask = inside(t)
+        return field(0, t) if mask is None else jnp.where(mask, field(0, t), 0.0)
+
+    def ice_of(t):
+        e = place(t)[1]
+        ice = mk[8 * e : 8 * e + 8, :] > 0 if t < strips else field(6, t) > 0.5
+        mask = inside(t)
+        return ice if mask is None else ice & mask
+
+    def keep(t, k, now):
+        vx[k, 8 * t : 8 * t + 8, :] = now
+
+    solve(strips + chunks, (coef, hb, w, w2), n_of, ice_of, field, keep)
+
+    def product(t):
+        at = slice(8 * t, 8 * t + 8)
+        return field(1, t) * (
+            w[0, at, :] * vx[0, at, :] + w[1, at, :] * vx[1, at, :]
         )
-        for t in range(LANES // 8):
-            unpack(
-                pl.ds(HALO + part * LANES + 8 * t, 8), turned[8 * t : 8 * t + 8, :]
-            )
-
-    def both(fn, *args):
-        return tuple(fn(*parts) for parts in zip(*args))
-
-    def down(x, kept):
-        turned = tuple(pltpu.roll(part, 1, 0) for part in x)
-        moved = both(lambda k, r: jnp.where(first_sub, k, r), kept, turned)
-        return moved, turned
-
-    side_inside = ((lane < 64) & (col < n_col - 1)) | ((lane >= 64) & (col > 0))
-    zero = jnp.zeros((8, LANES), jnp.float32)
-    add = functools.partial(both, lambda x, y: x + y)
-    sub_ = functools.partial(both, lambda x, y: x - y)
-
-    def rolls(x, by_lanes):
-        return tuple(pltpu.roll(part, by_lanes, 1) for part in x)
-
-    def from_next(x):
-        return jnp.where(last_lane, x[1], x[0]), jnp.where(last_lane, x[0], x[1])
-
-    def from_last(x):
-        return jnp.where(first_lane, x[1], x[0]), jnp.where(first_lane, x[0], x[1])
-
-    def store_state(to, t, k, now):
-        for i in range(2):
-            to[i, k, 8 * t : 8 * t + 8, :] = now[i]
-        return rolls(now, LANES - 1)
-
-    def store_ahead(to, t, k, turned):
-        ahead = from_next(turned)
-        for i in range(2):
-            to[i, 2 + k, 8 * t : 8 * t + 8, :] = ahead[i]
-
-    def store_both_ahead(to):
-        def stage(t, turned):
-            for k in range(2):
-                store_ahead(to, t, k, turned[k])
-
-        return stage
-
-    def open_(t, _):
-        at = pl.ds(8 * t, 8)
-        n = (fm[0, at, :], fs[0, at, :])
-        inside = (None, side_inside)
-        if t == 0 or t == chunks - 1:
-            there = line > 0 if t == 0 else line < n_line - 1
-            inside = (jnp.broadcast_to(there, (8, LANES)), side_inside & there)
-            n = (jnp.where(inside[0], n[0], 0.0), n[1])
-        n = (n[0], jnp.where(inside[1], n[1], 0.0))
-        return n, inside, rolls(n, 1)
-
-    summed_kept = [(zero, zero)]
-
-    def settle(t, given):
-        n, inside, turned = given
-        at = pl.ds(8 * t, 8)
-        ice = (mk[at, :] > 0, (fs[6, at, :] > 0.5) & inside[1])
-        if inside[0] is not None:
-            ice = (ice[0] & inside[0], ice[1])
-        summed = add(n, from_last(turned))
-        moved, summed_kept[0] = down(summed, summed_kept[0])
-        states = []
-        for i, source in ((0, fm), (1, fs)):
-            f = source[1, at, :]
-            half = jnp.where(
-                ice[i], 0.5 / (1.25 * (summed[i] + moved[i]) + f), 0.0
-            )
-            coef[i, 0, at, :] = 0.5 * n[i]
-            coef[i, 1, at, :] = 0.25 * n[i]
-            coef[i, 2, at, :] = half
-            coef[i, 3, at, :] = 1.0 - half * f
-            scaled = [half * source[2 + k, at, :] for k in range(2)]
-            for k in range(2):
-                hb[i, k, at, :] = scaled[k]
-            states.append([part + part for part in scaled])
-        return [store_state(w, t, k, (states[0][k], states[1][k])) for k in range(2)]
-
-    pipeline(chunks, LAG, open_, settle, store_both_ahead(w))
-    for i in range(2):
-        for k in range(4):
-            w[i, k, 8 * chunks : 8 * chunks + 8, :] = zero
-            w2[i, k, 8 * chunks : 8 * chunks + 8, :] = zero
-
-    def turn():
-        def begin(t, _):
-            at = pl.ds(8 * t, 8)
-            states = []
-            for k in range(2):
-                state = []
-                for i, source in ((0, fm), (1, fs)):
-                    now = w2[i, k, at, :]
-                    if i == 0 and 0 < t < chunks - 1:
-                        v[k, 8 * t - HALO : 8 * t - HALO + 8, :] = now
-                    scaled = coef[i, 2, at, :] * (now - source[4 + k, at, :])
-                    hb[i, k, at, :] = scaled
-                    state.append(scaled + scaled)
-                states.append(store_state(w2, t, k, tuple(state)))
-            return states
-
-        pipeline(chunks, LAG, begin, store_both_ahead(w2))
-
-    def sweep(w_from, w_to):
-        kept = [(zero, zero)] * 4
-
-        def pull(ref, k, at):
-            return ref[0, k, at, :], ref[1, k, at, :]
-
-        def front(t, _):
-            at, after = pl.ds(8 * t, 8), pl.ds(8 * t + 1, 8)
-            dx, dy = [], []
-            for k in range(2):
-                here, here_next = pull(w_from, k, at), pull(w_from, 2 + k, at)
-                below, below_next = pull(w_from, k, after), pull(w_from, 2 + k, after)
-                dx.append(add(sub_(below, here), sub_(below_next, here_next)))
-                dy.append(sub_(add(here_next, below_next), add(here, below)))
-            m, q = pull(coef, 0, at), pull(coef, 1, at)
-            total = add(dx[0], dy[1])
-            product = functools.partial(both, lambda a, b: a * b)
-            one = product(m, add(total, dx[0]))
-            two = product(m, add(total, dy[1]))
-            shear = product(q, add(dy[0], dx[1]))
-            fields = (
-                add(one, shear),
-                sub_(one, shear),
-                add(two, shear),
-                sub_(shear, two),
-            )
-            moved = []
-            for i in range(4):
-                got, kept[i] = down(fields[i], kept[i])
-                moved.append(got)
-            stay = (sub_(moved[1], fields[0]), sub_(moved[3], fields[2]))
-            go = (sub_(moved[0], fields[1]), sub_(moved[2], fields[3]))
-            return stay, tuple(rolls(x, 1) for x in go)
-
-        def close(t, given):
-            at = pl.ds(8 * t, 8)
-            turned = []
-            for k in range(2):
-                image = add(given[0][k], from_last(given[1][k]))
-                now = tuple(
-                    (coef[i, 3, at, :] * w_from[i, k, at, :] + hb[i, k, at, :])
-                    - coef[i, 2, at, :] * image[i]
-                    for i in range(2)
-                )
-                turned.append(store_state(w_to, t, k, now))
-            return turned
-
-        pipeline(chunks, LAG, front, close, store_both_ahead(w_to))
-
-    def pair(s, _):
-        sweep(w, w2)
-
-        @pl.when(s == 1)
-        def _():
-            turn()
-
-        sweep(w2, w)
-        return 0
-
-    lax.fori_loop(0, SWEEPS, pair, 0)
-
-    for t in range(TILE // 8):
-        total = None
-        for start in range(0, rows, TILE):
-            at = pl.ds(start + 8 * t, 8)
-            ext = pl.ds(HALO + start + 8 * t, 8)
-            piece = fm[1, ext, :] * (
-                w[0, 0, ext, :] * v[0, at, :] + w[0, 1, ext, :] * v[1, at, :]
-            )
-            total = piece if total is None else total + piece
-        dens[8 * t : 8 * t + 8, :] = -total
+
+    def merged(strip, turned, base):
+        return jnp.where(lane < 8, strip, jnp.where(lane >= 120, turned, base))
+
+    def strip_product(t, _):
+        strip = product(strips + 1 + t)
+        return strip, pltpu.roll(strip, 64, 1)
+
+    def put_product(t, given):
+        if t == 0 or t == rows // 8 - 1:
+            base = product(upper if t == 0 else lower)
+        else:
+            base = dm[8 * t : 8 * t + 8, :]
+        u = 8 * t % TILE
+        piece = merged(*given, base)
+        if 8 * t < TILE:
+            dens[u : u + 8, :] = -piece
+        else:
+            dens[u : u + 8, :] = dens[u : u + 8, :] - piece
+
+    pipeline(rows // 8, 8, strip_product, put_product)
 
     for copy in loads:
         copy.wait()
@@ -470,6 +535,26 @@
         to = by(0, 0, i)
         start(0, send_a.at[lax.rem(to["col"], SHARES)], recv_a.at[col], to)
     recv_a[col] = send_a[share]
+
+    def strip_velocity(t, _):
+        found = []
+        for k in range(2):
+            at = 8 * (strips + 1 + t)
+            strip = vx[k, at : at + 8, :]
+            found.append((strip, pltpu.roll(strip, 64, 1)))
+        return found
+
+    def put_velocity(t, given):
+        at = slice(8 * t, 8 * t + 8)
+        for k in range(2):
+            if t == 0 or t == rows // 8 - 1:
+                e = 8 * (upper if t == 0 else lower)
+                base = vx[k, e : e + 8, :]
+            else:
+                base = v_in[k, at, :]
+            v[k, at, :] = merged(*given[k], base)
+
+    pipeline(rows // 8, 8, strip_velocity, put_velocity)
     arrived(0, recv_a.at[0 : n_col - 1])
     total = recv_a[0]
     for i in range(1, n_col):
@@ -527,14 +612,21 @@
             out_shape=(
                 jax.ShapeDtypeStruct((6, ext, LANES), f32),
                 jax.ShapeDtypeStruct((ext, LANES), jnp.int32),
-                jax.ShapeDtypeStruct((8, 16, rows), f32),
+                jax.ShapeDtypeStruct((16, 8, rows), f32),
                 jax.ShapeDtypeStruct((4, 8, LANES), f32),
+                jax.ShapeDtypeStruct((FIELDS, rows, LANES), f32),
+                jax.ShapeDtypeStruct((2, rows, LANES), f32),
+                jax.ShapeDtypeStruct((rows, LANES), f32),
             ),
             in_specs=[hbm] * 5,
-            out_specs=[here] * 4,
+            out_specs=[here] * 7,
             scratch_shapes=[
                 vmem((rows, LANES), f32),
                 vmem((8, 16, rows), f32),
+                vmem((4, rows, LANES), f32),
+                vmem((2, rows, LANES), f32),
+                vmem((4, rows + 8, LANES), f32),
+                vmem((4, rows + 8, LANES), f32),
                 dma((5,)),
                 dma((10,)),
                 dma((10,)),
@@ -551,14 +643,15 @@
                 jax.ShapeDtypeStruct((2, rows, LANES), f32),
                 jax.ShapeDtypeStruct((1, per_owner, MODES * MODES), f32),
             ),
-            in_specs=[here] * 4 + [hbm] * 4,
+            in_specs=[here] * 7 + [hbm] * 4,
             out_specs=[here] * 2,
             scratch_shapes=[
                 vmem((FIELDS, ext, LANES), f32),
-                vmem((2, 4, ext, LANES), f32),
-                vmem((2, 2, ext, LANES), f32),
-                vmem((2, 4, ext + 8, LANES), f32),
-                vmem((2, 4, ext + 8, LANES), f32),
+                vmem((4, ext + 48, LANES), f32),
+                vmem((2, ext + 48, LANES), f32),
+                vmem((4, ext + 56, LANES), f32),
+                vmem((4, ext + 56, LANES), f32),
+                vmem((2, ext + 48, LANES), f32),
                 vmem((TILE, LANES), f32),
                 vmem(first.shape, f32),
                 vmem(second.shape, f32),

time: 40.5 us -> 39.1 us (0.965)
  Pallas kernels: 38.4 us -> 36.9 us
    pallas_call x1, Pallas kernels: 20.2 us -> 18.8 us  [local(): pl.pallas_call(functools.partial(kernel, sizes), out_shape=(jax.ShapeDtyp...]
where the time goes in v4:
time: 39.1 us; the launch traced here: 38.9 us
  Pallas kernels  36.9 us (94%)
  local copies, waits for them, and re-layouts  1.33 us (3%)
  between operations  0.65 us (2%)
    pallas_call x1, Pallas kernels, local(): pl.pallas_call(functools.partial(kernel, sizes), out_shape=(jax.ShapeDtyp...  18.8 us
    pallas_call x1, Pallas kernels, local(): pl.pallas_call(functools.partial(exchange, sizes), out_shape=(jax.ShapeDt...  18.2 us
    unnamed x2, local copies, waits for them, and re-layouts  1.33 us

profile of v4, /device:TPU:1, one launch (start us, length us, event | category | flops | bytes accessed | tf_op | source)
XLA Modules:
  0.0 38.9 jit_solution(6678474409918682287)
XLA Ops:
  0.6 18.2 %shard_map.104 = (f32[6,272,128]{2,1,0:T(8,128)S(1)}, s32[272,128]{1,0:T(8,128)S(1)}, f32[16,8,256]{2,1,0:T(8,128)S(1)}, f32[4,8,128]{2,1,0:T(8,128)S(1)}, f32[7...) custom-call(f32[256,128]{1,0:T(8,128)} %visc.1, f32[256,128]{1,0:T(8,128)} %fric.1, ...), custom_call_target="tpu_custom_call" | custom-call | tf_op jit(solution)/shard_map/pallas_call | solution.py:610
  18.8 18.8 %shard_map.105 = (f32[2,256,128]{2,1,0:T(8,128)S(1)}, f32[1,16,1024]{2,1,0:T(8,128)S(1)}) custom-call(f32[6,272,128]{2,1,0:T(8,128)S(1)} %get-tuple-element.9.fm, s32[272,128]{1,0:T(8,128)S(1)} %get-tuple-element.10.mk, f32[16,8,256]{2,1,0:T(8,128)S(1)} %get-tuple-element.11.recv_t, f32[4,8,128]{2,1,0:T(8,128)S(1)} %get-tuple-element.12.diag, ...), custom_call_target="tpu_custom_call" | custom-call | tf_op jit(solution)/shard_map/pallas_call | solution.py:640
  37.6 0.7 %copy.13 = f32[2,256,128]{2,1,0:T(8,128)} copy(f32[2,256,128]{2,1,0:T(8,128)S(1)} %get-tuple-element.18) | data formatting | bytes 524288
  38.3 0.6 %copy.14 = f32[1,16,1024]{2,1,0:T(8,128)} copy(f32[1,16,1024]{2,1,0:T(8,128)S(1)} %get-tuple-element.19) | data formatting | bytes 131072

commit v5 on v4

--- a/solution.py
+++ b/solution.py
@@ -163,165 +163,19 @@
     lax.fori_loop(0, SWEEPS, pair, 0)
 
 
-def exchange(
+def kernel(
     sizes,
     visc,
     fric,
     drv,
     obs,
     mask,
-    fm,
-    mk,
-    recv_t,
-    diag,
-    beside,
+    tile_block,
+    owner_list,
+    basis_1,
+    basis_2,
     v,
-    dm,
-    pack,
-    pack_t,
-    coef,
-    hb,
-    w,
-    w2,
-    load_sem,
-    halo_send,
-    halo_recv,
-):
-    n_row, n_own, n_col = sizes
-    n_line = n_row * n_own
-    rows = visc.shape[0]
-    row_at, own_at, col = (
-        lax.axis_index("row"),
-        lax.axis_index("own"),
-        lax.axis_index("col"),
-    )
-    line = row_at * n_own + own_at
-
-    def by(rows_on, owns_on, cols_on):
-        return {
-            "row": lax.rem(row_at + (rows_on + n_row), n_row),
-            "own": lax.rem(own_at + (owns_on + n_own), n_own),
-            "col": lax.rem(col + (cols_on + n_col), n_col),
-        }
-
-    def next_to(line_on, cols_on):
-        to = lax.rem(line + (line_on + n_line), n_line)
-        return {
-            "row": lax.div(to, n_own),
-            "own": lax.rem(to, n_own),
-            "col": lax.rem(col + (cols_on + n_col), n_col),
-        }
-
-    own_rows = pl.ds(HALO, rows)
-    loads = [
-        (visc, fm.at[0, own_rows, :]),
-        (fric, fm.at[1, own_rows, :]),
-        (drv, fm.at[2:4, own_rows, :]),
-        (obs, fm.at[4:6, own_rows, :]),
-        (mask, mk.at[own_rows, :]),
-    ]
-    loads = [
-        pltpu.make_async_copy(src, dst, load_sem.at[i])
-        for i, (src, dst) in enumerate(loads)
-    ]
-    for copy in loads:
-        copy.start()
-
-    barrier = pltpu.get_barrier_semaphore()
-    greeted = [next_to(i, j) for i in (-1, 1) for j in (-1, 0, 1)]
-    greeted += [by(0, 0, i) for i in (-1, 1)]
-    for to in greeted:
-        pl.semaphore_signal(barrier, inc=1, device_id=to, device_id_type=MESH)
-
-    lane = lax.broadcasted_iota(jnp.int32, (8, LANES), 1)
-
-    for copy in loads:
-        copy.wait()
-
-    def gather(t, _):
-        at = pl.ds(HALO + 8 * t, 8)
-        found = [fm[f, at, :] for f in range(6)] + [mk[at, :].astype(jnp.float32)]
-        return [pltpu.roll(piece, 16 * f + 8, 1) for f, piece in enumerate(found)]
-
-    def merge(t, pieces):
-        packed = pieces[0]
-        for f in range(1, FIELDS):
-            packed = jnp.where(lane < 16 * f, packed, pieces[f])
-        pack[8 * t : 8 * t + 8, :] = packed
-
-    pipeline(rows // 8, 4, gather, merge)
-    for part in range(rows // LANES):
-        block = pack[part * LANES : (part + 1) * LANES, :]
-        pack_t[:, :, part * LANES : (part + 1) * LANES] = block.T.reshape(8, 16, LANES)
-    recv_t[FIELDS : 16 - FIELDS] = jnp.zeros((2, 8, rows), jnp.float32)
-
-    pl.semaphore_wait(barrier, len(greeted))
-    copies = []
-
-    def send(src, dst, to):
-        at = len(copies)
-        copy = pltpu.make_async_remote_copy(
-            src_ref=src,
-            dst_ref=dst,
-            send_sem=halo_send.at[at],
-            recv_sem=halo_recv.at[at],
-            device_id=to,
-            device_id_type=MESH,
-        )
-        copy.start()
-        copies.append(copy)
-
-    for line_on, source, slot in ((-1, 0, 2), (1, rows - 8, 0)):
-        for cols_on in (-1, 1):
-            send(
-                pack.at[pl.ds(source, 8), :],
-                diag.at[slot + (1 if cols_on < 0 else 0)],
-                next_to(line_on, cols_on),
-            )
-    send(pack_t.at[0:FIELDS, 0:8, :], recv_t.at[0:FIELDS], by(0, 0, 1))
-    send(pack_t.at[0:FIELDS, 8:16, :], recv_t.at[16 - FIELDS : 16], by(0, 0, -1))
-    for line_on, source, target in ((-1, HALO, HALO + rows), (1, rows, 0)):
-        to, take = pl.ds(target, HALO), pl.ds(source, HALO)
-        send(fm.at[:, take, :], fm.at[:, to, :], next_to(line_on, 0))
-        send(mk.at[take, :], mk.at[to, :], next_to(line_on, 0))
-
-    def turn_half(t, _):
-        at = pl.ds(HALO + 8 * t, 8)
-        found = [fm[f, at, :] for f in range(6)] + [mk[at, :].astype(jnp.float32)]
-        return [(x, pltpu.roll(x, 64, 1)) for x in found]
-
-    def put_half(t, pieces):
-        for f, (x, turned) in enumerate(pieces):
-            beside[f, 8 * t : 8 * t + 8, :] = jnp.where(lane < 32, x, turned)
-
-    pipeline(rows // 8, 2, turn_half, put_half)
-
-    def field(f, t):
-        return fm[f, HALO + 8 * t : HALO + 8 * t + 8, :]
-
-    def keep(t, k, now):
-        v[k, 8 * t : 8 * t + 8, :] = now
-
-    solve(
-        rows // 8,
-        (coef, hb, w, w2),
-        lambda t: field(0, t),
-        lambda t: mk[HALO + 8 * t : HALO + 8 * t + 8, :] > 0,
-        field,
-        keep,
-    )
-    for t in range(1, rows // 8 - 1):
-        at = slice(8 * t, 8 * t + 8)
-        dm[at, :] = field(1, t) * (
-            w[0, at, :] * v[0, at, :] + w[1, at, :] * v[1, at, :]
-        )
-
-    for copy in copies:
-        copy.wait()
-
-
-def kernel(
-    sizes,
+    grad,
     fm,
     mk,
     recv_t,
@@ -329,12 +183,8 @@
     beside,
     v_in,
     dm,
-    tile_block,
-    owner_list,
-    basis_1,
-    basis_2,
-    v,
-    grad,
+    pack,
+    pack_t,
     fs,
     coef,
     hb,
@@ -350,12 +200,14 @@
     recv_a,
     table,
     load_sem,
+    halo_send,
+    halo_recv,
     phase_send,
     phase_recv,
 ):
     n_row, n_own, n_col = sizes
     n_line = n_row * n_own
-    rows = fm.shape[1] - 2 * HALO
+    rows = visc.shape[0]
     chunks = (rows + 2 * HALO) // 8
     row_at, own_at, col = (
         lax.axis_index("row"),
@@ -371,11 +223,32 @@
             "col": lax.rem(col + (cols_on + n_col), n_col),
         }
 
+    def next_to(line_on, cols_on):
+        to = lax.rem(line + (line_on + n_line), n_line)
+        return {
+            "row": lax.div(to, n_own),
+            "own": lax.rem(to, n_own),
+            "col": lax.rem(col + (cols_on + n_col), n_col),
+        }
+
     col_steps = sorted(range(1, n_col), key=lambda i: -around(i, n_col))
     plane_steps = [(i, j) for i in range(n_row) for j in range(n_own) if i or j]
     plane_steps.sort(key=lambda s: -(around(s[0], n_row) + around(s[1], n_own)))
 
+    barrier = pltpu.get_barrier_semaphore()
+    greeted = [by(i, j, 0) for i, j in plane_steps]
+    greeted += [by(0, 0, i) for i in col_steps]
+    greeted += [next_to(i, j) for i in (-1, 1) for j in (-1, 1)]
+    for to in greeted:
+        pl.semaphore_signal(barrier, inc=1, device_id=to, device_id_type=MESH)
+
+    own_rows = pl.ds(HALO, rows)
     loads = [
+        (visc, fm.at[0, own_rows, :]),
+        (fric, fm.at[1, own_rows, :]),
+        (drv, fm.at[2:4, own_rows, :]),
+        (obs, fm.at[4:6, own_rows, :]),
+        (mask, mk.at[own_rows, :]),
         (basis_1, b1),
         (basis_2, b2),
         (tile_block, tb),
@@ -388,13 +261,91 @@
     for copy in loads:
         copy.start()
 
-    barrier = pltpu.get_barrier_semaphore()
-    greeted = [by(0, 0, i) for i in col_steps]
-    greeted += [by(i, j, 0) for i, j in plane_steps]
-    for to in greeted:
-        pl.semaphore_signal(barrier, inc=1, device_id=to, device_id_type=MESH)
-
     lane = lax.broadcasted_iota(jnp.int32, (8, LANES), 1)
+
+    for copy in loads[:5]:
+        copy.wait()
+
+    def gather(t, _):
+        at = pl.ds(HALO + 8 * t, 8)
+        found = [fm[f, at, :] for f in range(6)] + [mk[at, :].astype(jnp.float32)]
+        return [pltpu.roll(piece, 16 * f + 8, 1) for f, piece in enumerate(found)]
+
+    def merge(t, pieces):
+        packed = pieces[0]
+        for f in range(1, FIELDS):
+            packed = jnp.where(lane < 16 * f, packed, pieces[f])
+        pack[8 * t : 8 * t + 8, :] = packed
+
+    pipeline(rows // 8, 4, gather, merge)
+    for part in range(rows // LANES):
+        block = pack[part * LANES : (part + 1) * LANES, :]
+        pack_t[:, :, part * LANES : (part + 1) * LANES] = block.T.reshape(8, 16, LANES)
+    recv_t[FIELDS : 16 - FIELDS] = jnp.zeros((2, 8, rows), jnp.float32)
+
+    pl.semaphore_wait(barrier, len(greeted))
+    copies = []
+
+    def send(src, dst, to):
+        at = len(copies)
+        copy = pltpu.make_async_remote_copy(
+            src_ref=src,
+            dst_ref=dst,
+            send_sem=halo_send.at[at],
+            recv_sem=halo_recv.at[at],
+            device_id=to,
+            device_id_type=MESH,
+        )
+        copy.start()
+        copies.append(copy)
+
+    for line_on, source, slot in ((-1, 0, 2), (1, rows - 8, 0)):
+        for cols_on in (-1, 1):
+            send(
+                pack.at[pl.ds(source, 8), :],
+                diag.at[slot + (1 if cols_on < 0 else 0)],
+                next_to(line_on, cols_on),
+            )
+    send(pack_t.at[0:FIELDS, 0:8, :], recv_t.at[0:FIELDS], by(0, 0, 1))
+    send(pack_t.at[0:FIELDS, 8:16, :], recv_t.at[16 - FIELDS : 16], by(0, 0, -1))
+    for line_on, source, target in ((-1, HALO, HALO + rows), (1, rows, 0)):
+        to, take = pl.ds(target, HALO), pl.ds(source, HALO)
+        send(fm.at[:, take, :], fm.at[:, to, :], next_to(line_on, 0))
+        send(mk.at[take, :], mk.at[to, :], next_to(line_on, 0))
+
+    def turn_half(t, _):
+        at = pl.ds(HALO + 8 * t, 8)
+        found = [fm[f, at, :] for f in range(6)] + [mk[at, :].astype(jnp.float32)]
+        return [(x, pltpu.roll(x, 64, 1)) for x in found]
+
+    def put_half(t, pieces):
+        for f, (x, turned) in enumerate(pieces):
+            beside[f, 8 * t : 8 * t + 8, :] = jnp.where(lane < 32, x, turned)
+
+    pipeline(rows // 8, 2, turn_half, put_half)
+
+    def block_field(f, t):
+        return fm[f, HALO + 8 * t : HALO + 8 * t + 8, :]
+
+    def block_keep(t, k, now):
+        v_in[k, 8 * t : 8 * t + 8, :] = now
+
+    solve(
+        rows // 8,
+        (coef, hb, w, w2),
+        lambda t: block_field(0, t),
+        lambda t: mk[HALO + 8 * t : HALO + 8 * t + 8, :] > 0,
+        block_field,
+        block_keep,
+    )
+    for t in range(1, rows // 8 - 1):
+        at = slice(8 * t, 8 * t + 8)
+        dm[at, :] = block_field(1, t) * (
+            w[0, at, :] * v_in[0, at, :] + w[1, at, :] * v_in[1, at, :]
+        )
+
+    for copy in copies:
+        copy.wait_recv()
 
     def corners(e, left, right):
         at = pl.ds(8 * e, 8)
@@ -496,7 +447,7 @@
 
     pipeline(rows // 8, 8, strip_product, put_product)
 
-    for copy in loads:
+    for copy in loads[5:]:
         copy.wait()
     first = jnp.dot(
         b1[...], dens[...], precision=HIGHEST, preferred_element_type=jnp.float32
@@ -529,7 +480,6 @@
     def departed(phase, ref):
         pltpu.make_async_copy(ref, ref, phase_send.at[phase]).wait()
 
-    pl.semaphore_wait(barrier, len(greeted))
     share = lax.rem(col, SHARES)
     for i in col_steps:
         to = by(0, 0, i)
@@ -581,6 +531,8 @@
         start(2, mine_c, mine_c, to)
     arrived(2, grad.at[0, :, 0 : (SHARES - 1) * width])
 
+    for copy in copies:
+        copy.wait_send()
     departed(0, recv_a.at[0 : n_col - 1])
     departed(1, table.at[0 : 2 * n_line - 2])
     departed(2, grad.at[0, :, 0 : (SHARES - 1) * width])
@@ -607,45 +559,24 @@
         def pinned(operands):
             return [pltpu.with_memory_space_constraint(x, pltpu.HBM) for x in operands]
 
-        padded = pl.pallas_call(
-            functools.partial(exchange, sizes),
-            out_shape=(
-                jax.ShapeDtypeStruct((6, ext, LANES), f32),
-                jax.ShapeDtypeStruct((ext, LANES), jnp.int32),
-                jax.ShapeDtypeStruct((16, 8, rows), f32),
-                jax.ShapeDtypeStruct((4, 8, LANES), f32),
-                jax.ShapeDtypeStruct((FIELDS, rows, LANES), f32),
-                jax.ShapeDtypeStruct((2, rows, LANES), f32),
-                jax.ShapeDtypeStruct((rows, LANES), f32),
-            ),
-            in_specs=[hbm] * 5,
-            out_specs=[here] * 7,
-            scratch_shapes=[
-                vmem((rows, LANES), f32),
-                vmem((8, 16, rows), f32),
-                vmem((4, rows, LANES), f32),
-                vmem((2, rows, LANES), f32),
-                vmem((4, rows + 8, LANES), f32),
-                vmem((4, rows + 8, LANES), f32),
-                dma((5,)),
-                dma((10,)),
-                dma((10,)),
-            ],
-            compiler_params=pltpu.CompilerParams(
-                collective_id=0,
-                has_side_effects=True,
-                vmem_limit_bytes=16 * 2**20,
-            ),
-        )(*pinned(fields))
         return pl.pallas_call(
             functools.partial(kernel, sizes),
             out_shape=(
                 jax.ShapeDtypeStruct((2, rows, LANES), f32),
                 jax.ShapeDtypeStruct((1, per_owner, MODES * MODES), f32),
             ),
-            in_specs=[here] * 7 + [hbm] * 4,
+            in_specs=[hbm] * 9,
             out_specs=[here] * 2,
             scratch_shapes=[
+                vmem((6, ext, LANES), f32),
+                vmem((ext, LANES), jnp.int32),
+                vmem((16, 8, rows), f32),
+                vmem((4, 8, LANES), f32),
+                vmem((FIELDS, rows, LANES), f32),
+                vmem((2, rows, LANES), f32),
+                vmem((rows, LANES), f32),
+                vmem((rows, LANES), f32),
+                vmem((8, 16, rows), f32),
                 vmem((FIELDS, ext, LANES), f32),
                 vmem((4, ext + 48, LANES), f32),
                 vmem((2, ext + 48, LANES), f32),
@@ -660,16 +591,18 @@
                 vmem((SHARES, 2 * 8 // SHARES, LANES), f32),
                 vmem((n_col, 2 * 8 // SHARES, LANES), f32),
                 vmem((2 * n_line, 8 // SHARES, LANES), f32),
-                dma((4,)),
+                dma((9,)),
+                dma((10,)),
+                dma((10,)),
                 dma((3,)),
                 dma((3,)),
             ],
             compiler_params=pltpu.CompilerParams(
-                collective_id=1,
+                collective_id=0,
                 has_side_effects=True,
                 vmem_limit_bytes=32 * 2**20,
             ),
-        )(*padded, *pinned(small))
+        )(*pinned(fields + small))
 
     return jax.shard_map(
         local,

time: 39.1 us -> 39.3 us (level)
    pallas_call x1, Pallas kernels: 18.8 us -> 37.2 us  [local(): pl.pallas_call(functools.partial(kernel, sizes), out_shape=(jax.ShapeDtyp...]
    pallas_call x1 -> x0, Pallas kernels: 18.2 us -> none  [local(): pl.pallas_call(functools.partial(exchange, sizes), out_shape=(jax.ShapeDt...]
where the time goes in v5:
time: 39.3 us; the launch traced here: 39.1 us
  Pallas kernels  37.2 us (95%)
  local copies, waits for them, and re-layouts  1.33 us (3%)
  between operations  0.64 us (2%)
    pallas_call x1, Pallas kernels, local(): pl.pallas_call(functools.partial(kernel, sizes), out_shape=(jax.ShapeDtyp...  37.2 us
    unnamed x2, local copies, waits for them, and re-layouts  1.33 us

profile of v5, /device:TPU:1, one launch (start us, length us, event | category | flops | bytes accessed | tf_op | source)
XLA Modules:
  0.0 39.1 jit_solution(14002172693438972602)
XLA Ops:
  0.6 37.2 %shard_map.104 = (f32[2,256,128]{2,1,0:T(8,128)S(1)}, f32[1,16,1024]{2,1,0:T(8,128)S(1)}) custom-call(f32[256,128]{1,0:T(8,128)} %visc.1, f32[256,128]{1,0:T(8,128)} %fric.1, f32[2,256,128]{2,1,0:T(8,128)} %drv.1, f32[2,256,128]{2,1,0:T(8,128)} %obs.1, s32[256,128]{1,0:T(8,128)} %mask.1, s32[1,2]{1,0:T(1,128)} %bitcast.1, s32[64]{0:T(128)} %owner_list.1, ...), custom_call_target="tpu_custom_call" | custom-call | tf_op jit(solution)/shard_map/pallas_call | solution.py:562
  37.8 0.7 %copy.13 = f32[2,256,128]{2,1,0:T(8,128)} copy(f32[2,256,128]{2,1,0:T(8,128)S(1)} %get-tuple-element.4) | data formatting | bytes 524288
  38.5 0.6 %copy.14 = f32[1,16,1024]{2,1,0:T(8,128)} copy(f32[1,16,1024]{2,1,0:T(8,128)S(1)} %get-tuple-element.5) | data formatting | bytes 131072

commit v6 on v5

--- a/solution.py
+++ b/solution.py
@@ -27,9 +27,7 @@
     orders = np.arange(MODES)
     cosine = np.cos(math.pi * orders[:, None] * places[None, :] / TILE)
     first = np.concatenate([cosine[s::PER] for s in range(PER)], axis=0)
-    second = np.zeros((PER * TILE, LANES))
-    for s in range(PER):
-        second[s * TILE : (s + 1) * TILE, s * MODES : (s + 1) * MODES] = cosine.T / TILE
+    second = np.concatenate([cosine.T / TILE] * PER, axis=1)
     return first.astype(np.float32), second.astype(np.float32)
 
 
@@ -452,10 +450,12 @@
     first = jnp.dot(
         b1[...], dens[...], precision=HIGHEST, preferred_element_type=jnp.float32
     )
-    first = jnp.concatenate([first[8 * i : 8 * i + 8] for i in range(PER)], axis=1)
-    part = jnp.dot(
+    product_ = jnp.dot(
         first, b2[...], precision=HIGHEST, preferred_element_type=jnp.float32
     )
+    part = product_[0:8]
+    for i in range(1, PER):
+        part = jnp.where(lane < i * MODES, part, product_[8 * i : 8 * i + 8])
     in_second = tb[0, 0] > 2 * line
     parts = jnp.where(in_second, 0.0, part), jnp.where(in_second, part, 0.0)
     per_share = 8 // SHARES
@@ -536,6 +536,17 @@
     departed(0, recv_a.at[0 : n_col - 1])
     departed(1, table.at[0 : 2 * n_line - 2])
     departed(2, grad.at[0, :, 0 : (SHARES - 1) * width])
+
+
+def write_out(velocity, gradient, to_velocity, to_gradient, sem):
+    copies = [
+        pltpu.make_async_copy(velocity, to_velocity, sem.at[0]),
+        pltpu.make_async_copy(gradient, to_gradient, sem.at[1]),
+    ]
+    for copy in copies:
+        copy.start()
+    for copy in copies:
+        copy.wait()
 
 
 def solution(mesh):
@@ -559,7 +570,7 @@
         def pinned(operands):
             return [pltpu.with_memory_space_constraint(x, pltpu.HBM) for x in operands]
 
-        return pl.pallas_call(
+        results = pl.pallas_call(
             functools.partial(kernel, sizes),
             out_shape=(
                 jax.ShapeDtypeStruct((2, rows, LANES), f32),
@@ -603,6 +614,14 @@
                 vmem_limit_bytes=32 * 2**20,
             ),
         )(*pinned(fields + small))
+        return pl.pallas_call(
+            write_out,
+            out_shape=[jax.ShapeDtypeStruct(x.shape, f32) for x in results],
+            in_specs=[here] * 2,
+            out_specs=[hbm] * 2,
+            scratch_shapes=[dma((2,))],
+            compiler_params=pltpu.CompilerParams(vmem_limit_bytes=2**20),
+        )(*results)
 
     return jax.shard_map(
         local,

time: 39.3 us -> 38.6 us (0.982)
  local copies, waits for them, and re-layouts: 1.33 us -> 0 us
  Pallas kernels: 37.2 us -> 37.8 us
    unnamed x2 -> x0, local copies, waits for them, and re-layouts: 1.33 us -> none
    pallas_call x0 -> x1, Pallas kernels: none -> 0.74 us  [local(): pl.pallas_call(write_out, out_shape=[jax.ShapeDtypeStruct(x.shape, f32) f...]
where the time goes in v6:
time: 38.6 us; the launch traced here: 38.5 us
  Pallas kernels  37.8 us (98%)
  between operations  0.64 us (2%)
    pallas_call x1, Pallas kernels, local(): pl.pallas_call(functools.partial(kernel, sizes), out_shape=(jax.ShapeDtyp...  37.1 us

profile of v6, /device:TPU:1, one launch (start us, length us, event | category | flops | bytes accessed | tf_op | source)
XLA Modules:
  0.0 38.5 jit_solution(7218745101663279528)
XLA Ops:
  0.6 37.1 %shard_map.104 = (f32[2,256,128]{2,1,0:T(8,128)S(1)}, f32[1,16,1024]{2,1,0:T(8,128)S(1)}) custom-call(f32[256,128]{1,0:T(8,128)} %visc.1, f32[256,128]{1,0:T(8,128)} %fric.1, f32[2,256,128]{2,1,0:T(8,128)} %drv.1, f32[2,256,128]{2,1,0:T(8,128)} %obs.1, s32[256,128]{1,0:T(8,128)} %mask.1, s32[1,2]{1,0:T(1,128)} %bitcast.1, s32[64]{0:T(128)} %owner_list.1, ...), custom_call_target="tpu_custom_call" | custom-call | tf_op jit(solution)/shard_map/pallas_call | solution.py:573
  37.7 0.7 %shard_map.105 = (f32[2,256,128]{2,1,0:T(8,128)}, f32[1,16,1024]{2,1,0:T(8,128)}) custom-call(f32[2,256,128]{2,1,0:T(8,128)S(1)} %get-tuple-element.4.velocity, f32[1,16,1024]{2,1,0:T(8,128)S(1)} %get-tuple-element.5.gradient), custom_call_target="tpu_custom_call" | custom-call | tf_op jit(solution)/shard_map/pallas_call | solution.py:617

commit v7 on v6

--- a/solution.py
+++ b/solution.py
@@ -33,6 +33,18 @@
 
 def around(step, size):
     return min(step % size, -step % size)
+
+
+def wrapped(x, size):
+    if size & (size - 1) == 0:
+        return lax.bitwise_and(x, size - 1)
+    return lax.rem(x + size, size)
+
+
+def quotient(x, size):
+    if size & (size - 1) == 0:
+        return lax.shift_right_logical(x, size.bit_length() - 1)
+    return lax.div(x, size)
 
 
 def pipeline(count, lag, *stages):
@@ -214,19 +226,27 @@
     )
     line = row_at * n_own + own_at
 
+    row_by = [wrapped(row_at + i, n_row) for i in range(n_row)]
+    own_by = [wrapped(own_at + i, n_own) for i in range(n_own)]
+    col_by = [wrapped(col + i, n_col) for i in range(n_col)]
+
     def by(rows_on, owns_on, cols_on):
         return {
-            "row": lax.rem(row_at + (rows_on + n_row), n_row),
-            "own": lax.rem(own_at + (owns_on + n_own), n_own),
-            "col": lax.rem(col + (cols_on + n_col), n_col),
+            "row": row_by[rows_on],
+            "own": own_by[owns_on],
+            "col": col_by[cols_on],
         }
 
+    line_by = {i: wrapped(line + i, n_line) for i in (-1, 1)}
+    line_by = {
+        i: (quotient(to, n_own), wrapped(to, n_own)) for i, to in line_by.items()
+    }
+
     def next_to(line_on, cols_on):
-        to = lax.rem(line + (line_on + n_line), n_line)
         return {
-            "row": lax.div(to, n_own),
-            "own": lax.rem(to, n_own),
-            "col": lax.rem(col + (cols_on + n_col), n_col),
+            "row": line_by[line_on][0],
+            "own": line_by[line_on][1],
+            "col": col_by[cols_on],
         }
 
     col_steps = sorted(range(1, n_col), key=lambda i: -around(i, n_col))
@@ -480,10 +500,10 @@
     def departed(phase, ref):
         pltpu.make_async_copy(ref, ref, phase_send.at[phase]).wait()
 
-    share = lax.rem(col, SHARES)
+    share = wrapped(col, SHARES)
     for i in col_steps:
         to = by(0, 0, i)
-        start(0, send_a.at[lax.rem(to["col"], SHARES)], recv_a.at[col], to)
+        start(0, send_a.at[wrapped(to["col"], SHARES)], recv_a.at[col], to)
     recv_a[col] = send_a[share]
 
     def strip_velocity(t, _):

time: 38.6 us -> 38.6 us (level)
  no operation moved by 1% of the time
where the time goes in v7:
time: 38.6 us; the launch traced here: 38.5 us
  Pallas kernels  37.8 us (98%)
  between operations  0.64 us (2%)
    pallas_call x1, Pallas kernels, local(): pl.pallas_call(functools.partial(kernel, sizes), out_shape=(jax.ShapeDtyp...  37.1 us

profile of v7, /device:TPU:1, one launch (start us, length us, event | category | flops | bytes accessed | tf_op | source)
XLA Modules:
  0.0 38.5 jit_solution(9932532925695345036)
XLA Ops:
  0.6 37.1 %shard_map.104 = (f32[2,256,128]{2,1,0:T(8,128)S(1)}, f32[1,16,1024]{2,1,0:T(8,128)S(1)}) custom-call(f32[256,128]{1,0:T(8,128)} %visc.1, f32[256,128]{1,0:T(8,128)} %fric.1, f32[2,256,128]{2,1,0:T(8,128)} %drv.1, f32[2,256,128]{2,1,0:T(8,128)} %obs.1, s32[256,128]{1,0:T(8,128)} %mask.1, s32[1,2]{1,0:T(1,128)} %bitcast.1, s32[64]{0:T(128)} %owner_list.1, ...), custom_call_target="tpu_custom_call" | custom-call | tf_op jit(solution)/shard_map/pallas_call | solution.py:593
  37.7 0.7 %shard_map.105 = (f32[2,256,128]{2,1,0:T(8,128)}, f32[1,16,1024]{2,1,0:T(8,128)}) custom-call(f32[2,256,128]{2,1,0:T(8,128)S(1)} %get-tuple-element.4.velocity, f32[1,16,1024]{2,1,0:T(8,128)S(1)} %get-tuple-element.5.gradient), custom_call_target="tpu_custom_call" | custom-call | tf_op jit(solution)/shard_map/pallas_call | solution.py:637

commit v8 on v4

--- a/solution.py
+++ b/solution.py
@@ -27,14 +27,24 @@
     orders = np.arange(MODES)
     cosine = np.cos(math.pi * orders[:, None] * places[None, :] / TILE)
     first = np.concatenate([cosine[s::PER] for s in range(PER)], axis=0)
-    second = np.zeros((PER * TILE, LANES))
-    for s in range(PER):
-        second[s * TILE : (s + 1) * TILE, s * MODES : (s + 1) * MODES] = cosine.T / TILE
+    second = np.concatenate([cosine.T / TILE] * PER, axis=1)
     return first.astype(np.float32), second.astype(np.float32)
 
 
 def around(step, size):
     return min(step % size, -step % size)
+
+
+def wrapped(x, size):
+    if size & (size - 1) == 0:
+        return lax.bitwise_and(x, size - 1)
+    return lax.rem(x + size, size)
+
+
+def quotient(x, size):
+    if size & (size - 1) == 0:
+        return lax.shift_right_logical(x, size.bit_length() - 1)
+    return lax.div(x, size)
 
 
 def pipeline(count, lag, *stages):
@@ -197,19 +207,27 @@
     )
     line = row_at * n_own + own_at
 
+    row_by = [wrapped(row_at + i, n_row) for i in range(n_row)]
+    own_by = [wrapped(own_at + i, n_own) for i in range(n_own)]
+    col_by = [wrapped(col + i, n_col) for i in range(n_col)]
+
     def by(rows_on, owns_on, cols_on):
         return {
-            "row": lax.rem(row_at + (rows_on + n_row), n_row),
-            "own": lax.rem(own_at + (owns_on + n_own), n_own),
-            "col": lax.rem(col + (cols_on + n_col), n_col),
+            "row": row_by[rows_on],
+            "own": own_by[owns_on],
+            "col": col_by[cols_on],
         }
 
+    line_by = {i: wrapped(line + i, n_line) for i in (-1, 1)}
+    line_by = {
+        i: (quotient(to, n_own), wrapped(to, n_own)) for i, to in line_by.items()
+    }
+
     def next_to(line_on, cols_on):
-        to = lax.rem(line + (line_on + n_line), n_line)
         return {
-            "row": lax.div(to, n_own),
-            "own": lax.rem(to, n_own),
-            "col": lax.rem(col + (cols_on + n_col), n_col),
+            "row": line_by[line_on][0],
+            "own": line_by[line_on][1],
+            "col": col_by[cols_on],
         }
 
     own_rows = pl.ds(HALO, rows)
@@ -364,16 +382,26 @@
     )
     line = row_at * n_own + own_at
 
+    row_by = [wrapped(row_at + i, n_row) for i in range(n_row)]
+    own_by = [wrapped(own_at + i, n_own) for i in range(n_own)]
+    col_by = [wrapped(col + i, n_col) for i in range(n_col)]
+
     def by(rows_on, owns_on, cols_on):
         return {
-            "row": lax.rem(row_at + (rows_on + n_row), n_row),
-            "own": lax.rem(own_at + (owns_on + n_own), n_own),
-            "col": lax.rem(col + (cols_on + n_col), n_col),
+            "row": row_by[rows_on],
+            "own": own_by[owns_on],
+            "col": col_by[cols_on],
         }
 
     col_steps = sorted(range(1, n_col), key=lambda i: -around(i, n_col))
     plane_steps = [(i, j) for i in range(n_row) for j in range(n_own) if i or j]
     plane_steps.sort(key=lambda s: -(around(s[0], n_row) + around(s[1], n_own)))
+
+    barrier = pltpu.get_barrier_semaphore()
+    greeted = [by(i, j, 0) for i, j in plane_steps]
+    greeted += [by(0, 0, i) for i in col_steps]
+    for to in greeted:
+        pl.semaphore_signal(barrier, inc=1, device_id=to, device_id_type=MESH)
 
     loads = [
         (basis_1, b1),
@@ -388,12 +416,6 @@
     for copy in loads:
         copy.start()
 
-    barrier = pltpu.get_barrier_semaphore()
-    greeted = [by(0, 0, i) for i in col_steps]
-    greeted += [by(i, j, 0) for i, j in plane_steps]
-    for to in greeted:
-        pl.semaphore_signal(barrier, inc=1, device_id=to, device_id_type=MESH)
-
     lane = lax.broadcasted_iota(jnp.int32, (8, LANES), 1)
 
     def corners(e, left, right):
@@ -501,10 +523,12 @@
     first = jnp.dot(
         b1[...], dens[...], precision=HIGHEST, preferred_element_type=jnp.float32
     )
-    first = jnp.concatenate([first[8 * i : 8 * i + 8] for i in range(PER)], axis=1)
-    part = jnp.dot(
+    product_ = jnp.dot(
         first, b2[...], precision=HIGHEST, preferred_element_type=jnp.float32
     )
+    part = product_[0:8]
+    for i in range(1, PER):
+        part = jnp.where(lane < i * MODES, part, product_[8 * i : 8 * i + 8])
     in_second = tb[0, 0] > 2 * line
     parts = jnp.where(in_second, 0.0, part), jnp.where(in_second, part, 0.0)
     per_share = 8 // SHARES
@@ -530,10 +554,10 @@
         pltpu.make_async_copy(ref, ref, phase_send.at[phase]).wait()
 
     pl.semaphore_wait(barrier, len(greeted))
-    share = lax.rem(col, SHARES)
+    share = wrapped(col, SHARES)
     for i in col_steps:
         to = by(0, 0, i)
-        start(0, send_a.at[lax.rem(to["col"], SHARES)], recv_a.at[col], to)
+        start(0, send_a.at[wrapped(to["col"], SHARES)], recv_a.at[col], to)
     recv_a[col] = send_a[share]
 
     def strip_velocity(t, _):
@@ -584,6 +608,17 @@
     departed(0, recv_a.at[0 : n_col - 1])
     departed(1, table.at[0 : 2 * n_line - 2])
     departed(2, grad.at[0, :, 0 : (SHARES - 1) * width])
+
+
+def write_out(velocity, gradient, to_velocity, to_gradient, sem):
+    copies = [
+        pltpu.make_async_copy(velocity, to_velocity, sem.at[0]),
+        pltpu.make_async_copy(gradient, to_gradient, sem.at[1]),
+    ]
+    for copy in copies:
+        copy.start()
+    for copy in copies:
+        copy.wait()
 
 
 def solution(mesh):
@@ -637,7 +672,7 @@
                 vmem_limit_bytes=16 * 2**20,
             ),
         )(*pinned(fields))
-        return pl.pallas_call(
+        results = pl.pallas_call(
             functools.partial(kernel, sizes),
             out_shape=(
                 jax.ShapeDtypeStruct((2, rows, LANES), f32),
@@ -670,6 +705,14 @@
                 vmem_limit_bytes=32 * 2**20,
             ),
         )(*padded, *pinned(small))
+        return pl.pallas_call(
+            write_out,
+            out_shape=[jax.ShapeDtypeStruct(x.shape, f32) for x in results],
+            in_specs=[here] * 2,
+            out_specs=[hbm] * 2,
+            scratch_shapes=[dma((2,))],
+            compiler_params=pltpu.CompilerParams(vmem_limit_bytes=2**20),
+        )(*results)
 
     return jax.shard_map(
         local,

time: 39.1 us -> 38.4 us (0.982)
  local copies, waits for them, and re-layouts: 1.33 us -> 0 us
  Pallas kernels: 36.9 us -> 37.6 us
    unnamed x2 -> x0, local copies, waits for them, and re-layouts: 1.33 us -> none
    pallas_call x0 -> x1, Pallas kernels: none -> 0.74 us  [local(): pl.pallas_call(write_out, out_shape=[jax.ShapeDtypeStruct(x.shape, f32) f...]
where the time goes in v8:
time: 38.4 us; the launch traced here: 38.2 us
  Pallas kernels  37.6 us (98%)
  between operations  0.65 us (2%)
    pallas_call x1, Pallas kernels, local(): pl.pallas_call(functools.partial(kernel, sizes), out_shape=(jax.ShapeDtyp...  18.7 us
    pallas_call x1, Pallas kernels, local(): pl.pallas_call(functools.partial(exchange, sizes), out_shape=(jax.ShapeDt...  18.1 us

profile of v8, /device:TPU:1, one launch (start us, length us, event | category | flops | bytes accessed | tf_op | source)
XLA Modules:
  0.0 38.2 jit_solution(7000234654834662088)
XLA Ops:
  0.6 18.1 %shard_map.104 = (f32[6,272,128]{2,1,0:T(8,128)S(1)}, s32[272,128]{1,0:T(8,128)S(1)}, f32[16,8,256]{2,1,0:T(8,128)S(1)}, f32[4,8,128]{2,1,0:T(8,128)S(1)}, f32[7...) custom-call(f32[256,128]{1,0:T(8,128)} %visc.1, f32[256,128]{1,0:T(8,128)} %fric.1, ...), custom_call_target="tpu_custom_call" | custom-call | tf_op jit(solution)/shard_map/pallas_call | solution.py:645
  18.8 18.7 %shard_map.105 = (f32[2,256,128]{2,1,0:T(8,128)S(1)}, f32[1,16,1024]{2,1,0:T(8,128)S(1)}) custom-call(f32[6,272,128]{2,1,0:T(8,128)S(1)} %get-tuple-element.11.fm, s32[272,128]{1,0:T(8,128)S(1)} %get-tuple-element.12.mk, f32[16,8,256]{2,1,0:T(8,128)S(1)} %get-tuple-element.13.recv_t, f32[4,8,128]{2,1,0:T(8,128)S(1)} %get-tuple-element.14.diag, ...), custom_call_target="tpu_custom_call" | custom-call | tf_op jit(solution)/shard_map/pallas_call | solution.py:675
  37.5 0.7 %shard_map.106 = (f32[2,256,128]{2,1,0:T(8,128)}, f32[1,16,1024]{2,1,0:T(8,128)}) custom-call(f32[2,256,128]{2,1,0:T(8,128)S(1)} %get-tuple-element.18.velocity, f32[1,16,1024]{2,1,0:T(8,128)S(1)} %get-tuple-element.19.gradient), custom_call_target="tpu_custom_call" | custom-call | tf_op jit(solution)/shard_map/pallas_call | solution.py:708

commit v9 on v8

--- a/solution.py
+++ b/solution.py
@@ -230,6 +230,12 @@
             "col": col_by[cols_on],
         }
 
+    barrier = pltpu.get_barrier_semaphore()
+    greeted = [next_to(i, j) for i in (-1, 1) for j in (-1, 0, 1)]
+    greeted += [by(0, 0, i) for i in (-1, 1)]
+    for to in greeted:
+        pl.semaphore_signal(barrier, inc=1, device_id=to, device_id_type=MESH)
+
     own_rows = pl.ds(HALO, rows)
     loads = [
         (visc, fm.at[0, own_rows, :]),
@@ -244,12 +250,6 @@
     ]
     for copy in loads:
         copy.start()
-
-    barrier = pltpu.get_barrier_semaphore()
-    greeted = [next_to(i, j) for i in (-1, 1) for j in (-1, 0, 1)]
-    greeted += [by(0, 0, i) for i in (-1, 1)]
-    for to in greeted:
-        pl.semaphore_signal(barrier, inc=1, device_id=to, device_id_type=MESH)
 
     lane = lax.broadcasted_iota(jnp.int32, (8, LANES), 1)
 

time: 38.4 us -> 38.4 us (level)
  no operation moved by 1% of the time
where the time goes in v9:
time: 38.4 us; the launch traced here: 38.2 us
  Pallas kernels  37.6 us (98%)
  between operations  0.65 us (2%)
    pallas_call x1, Pallas kernels, local(): pl.pallas_call(functools.partial(kernel, sizes), out_shape=(jax.ShapeDtyp...  18.7 us
    pallas_call x1, Pallas kernels, local(): pl.pallas_call(functools.partial(exchange, sizes), out_shape=(jax.ShapeDt...  18.1 us

profile of v9, /device:TPU:1, one launch (start us, length us, event | category | flops | bytes accessed | tf_op | source)
XLA Modules:
  0.0 38.2 jit_solution(12622547946260642419)
XLA Ops:
  0.6 18.1 %shard_map.104 = (f32[6,272,128]{2,1,0:T(8,128)S(1)}, s32[272,128]{1,0:T(8,128)S(1)}, f32[16,8,256]{2,1,0:T(8,128)S(1)}, f32[4,8,128]{2,1,0:T(8,128)S(1)}, f32[7...) custom-call(f32[256,128]{1,0:T(8,128)} %visc.1, f32[256,128]{1,0:T(8,128)} %fric.1, ...), custom_call_target="tpu_custom_call" | custom-call | tf_op jit(solution)/shard_map/pallas_call | solution.py:645
  18.8 18.7 %shard_map.105 = (f32[2,256,128]{2,1,0:T(8,128)S(1)}, f32[1,16,1024]{2,1,0:T(8,128)S(1)}) custom-call(f32[6,272,128]{2,1,0:T(8,128)S(1)} %get-tuple-element.11.fm, s32[272,128]{1,0:T(8,128)S(1)} %get-tuple-element.12.mk, f32[16,8,256]{2,1,0:T(8,128)S(1)} %get-tuple-element.13.recv_t, f32[4,8,128]{2,1,0:T(8,128)S(1)} %get-tuple-element.14.diag, ...), custom_call_target="tpu_custom_call" | custom-call | tf_op jit(solution)/shard_map/pallas_call | solution.py:675
  37.5 0.7 %shard_map.106 = (f32[2,256,128]{2,1,0:T(8,128)}, f32[1,16,1024]{2,1,0:T(8,128)}) custom-call(f32[2,256,128]{2,1,0:T(8,128)S(1)} %get-tuple-element.18.velocity, f32[1,16,1024]{2,1,0:T(8,128)S(1)} %get-tuple-element.19.gradient), custom_call_target="tpu_custom_call" | custom-call | tf_op jit(solution)/shard_map/pallas_call | solution.py:708
